TPU v7x, 128 devices: a whole 4x4x4 slice. The times are simulated.
128 devices in a mesh: blk: 64 (over z, x_lo, y, core), head: 2 (over x_hi).
Axes of the slice: x: 4 (x_hi: 2, x_lo: 2; x = x_hi * 2 + x_lo), y: 4, z: 4, core: 2. Of those that a mesh axis runs over, the one named last changes fastest.
Arguments:
- tokens: bfloat16 [16384, 512], P('blk'), may hold values from -6 to 6
- cotangents: bfloat16 [2, 16384, 512], P(None, 'blk'), may hold values from -24 to 24
- segment_ids: int32 [16384], P('blk'), may hold values from 0 to 256, as said below
- in_weights: bfloat16 [3, 512, 512], P(None, None, 'head'), may hold values from -0.25 to 0.25
- in_biases: float32 [2, 512], P(None, 'head'), may hold values from -3 to 3
- out_weight: bfloat16 [512, 512], P('head'), may hold values from -6 to 6
- up_weight: bfloat16 [512, 2048], P(None, 'head'), may hold values from -0.25 to 0.25
- up_biases: float32 [2048], P('head'), may hold values from -3 to 3
- down_weight: bfloat16 [2048, 512], P('head'), may hold values from -0.125 to 0.125
- gains: float32 [2, 512], replicated, may hold values from 0.1 to 1.9
- shifts: float32 [4, 512], replicated, may hold values from -3 to 3
Outputs:
- mixed: bfloat16 [16384, 512], P('blk')
- grad_tokens: float32 [2, 16384, 512], P(None, 'blk')
- grad_in_weights: float32 [2, 3, 512, 512], P(None, None, None, 'head')
- grad_in_biases: float32 [2, 2, 512], P(None, None, 'head')
- grad_out_weight: float32 [2, 512, 512], P(None, 'head')
- grad_up_weight: float32 [2, 512, 2048], P(None, None, 'head')
- grad_up_biases: float32 [2, 2048], P(None, 'head')
- grad_down_weight: float32 [2, 2048, 512], P(None, 'head')
- grad_gains: float32 [2, 2, 512], replicated
- grad_shifts: float32 [2, 4, 512], replicated
Inputs may be any that keep to these rules, and one draw needn't show every extreme that they name: `segment_ids`: id 0 is one image: in every block of 256 rows of one device its tokens come first, 64 times a number from 1 to 3 of them; in every draw some device holds 192 image tokens and another holds 64. Every other token has the id 1 + its position // 64, so each thumbnail is 64 tokens on one device.
All inputs are finite; a program needn't handle non-finite values.
Results may differ from a plain program's by a relative error of at most 0.025.
Values may be sent and summed in bfloat16 or wider, within the bound.
No kernel may reach another device: no remote copies, remote signals or barrier semaphores. Data moves between devices by JAX's collectives and lax.ppermute only.
A program may use at most 320 MiB of HBM per device.

v0:
```python
import functools

import jax
import jax.numpy as jnp
from jax import lax
from jax.experimental import pallas as pl
from jax.experimental.pallas import tpu as pltpu
from jax.sharding import Mesh
from jax.sharding import PartitionSpec as P

HD = 64
LANES = 128
TILE = 64
BLOCK = 256
EPS = 1e-06
SCALE = 0.125
FAR = -1e30
BF = jnp.bfloat16
F32 = jnp.float32
MIB = 1024 * 1024
ROOM = 56

NT = (((1,), (1,)), ((), ()))
TN = (((0,), (0,)), ((), ()))


def shift_by(array, axis, step):
    size = lax.axis_size(axis)
    return lax.ppermute(array, axis, [(i, (i + step) % size) for i in range(size)])


def dot(a, b):
    return jnp.dot(a, b, preferred_element_type=F32)


def dot_nt(a, b):
    return lax.dot_general(a, b, NT, preferred_element_type=F32)


def dot_tn(a, b):
    return lax.dot_general(a, b, TN, preferred_element_type=F32)


def standard(field):
    center = field - jnp.mean(field, axis=-1, keepdims=True)
    factor = lax.rsqrt(jnp.mean(center * center, axis=-1, keepdims=True) + EPS)
    return center * factor, factor


def norm_back(grad, gain, xhat, factor):
    h = grad * gain
    mean = jnp.mean(h, axis=-1, keepdims=True)
    return factor * (h - mean - xhat * jnp.mean(h * xhat, axis=-1, keepdims=True))


def pieces(value):
    high = value.astype(BF)
    rest = value - high.astype(F32)
    middle = rest.astype(BF)
    low = (rest - middle.astype(F32)).astype(BF)
    return high, middle, low


def zero_one(mask):
    return jnp.where(mask, 1.0, 0.0).astype(BF)


def iota(shape, dim):
    return lax.broadcasted_iota(jnp.int32, shape, dim)


VMEM = pl.BlockSpec(memory_space=pltpu.VMEM)
ANY = pl.BlockSpec(memory_space=pl.ANY)
SMEM = pl.BlockSpec(memory_space=pltpu.SMEM)


def local_call(body, name, out, ins, outs, args, scratch=(), cost=None, room=16):
    return pl.pallas_call(
        body,
        out_shape=out,
        in_specs=ins,
        out_specs=outs,
        scratch_shapes=scratch,
        cost_estimate=cost,
        compiler_params=pltpu.CompilerParams(vmem_limit_bytes=room * MIB),
        name=name,
    )(*args)


def shaped(*shape, dtype=BF):
    return jax.ShapeDtypeStruct(shape, dtype)


def cost(micros):
    return pl.CostEstimate(flops=int(micros * 1e9), bytes_accessed=0, transcendentals=0)


def front_kernel(tokens, ids, told, copies, number):
    rows = told.shape[0] - 16
    marks = jnp.where(ids[...] == 0, 1.0, 0.0)
    tiles = jnp.sum(marks).astype(jnp.int32) // TILE
    number[0] = tiles
    told[:rows, :] = tokens[:rows, :]
    told[rows:, :] = jnp.full((16, told.shape[1]), tiles.astype(F32), F32).astype(BF)
    for g in range(copies.shape[0]):
        copies[g] = told[...]


def front(tokens, ids, copies):
    size, model = tokens.shape
    told = size - TILE + 16
    return local_call(
        front_kernel,
        "front",
        (shaped(told, model), shaped(copies, told, model), shaped(1, dtype=jnp.int32)),
        [VMEM, VMEM],
        (VMEM, VMEM, SMEM),
        (tokens, ids.reshape(-1, LANES)),
        room=ROOM,
    )


def prepare_kernel(
    heads, place, in_weights, in_biases, gains, shifts, up, down, bias,
    weights, biases, pairs, columns, out,
):
    core = place[0]
    half = out.shape[1]
    at = pl.ds(pl.multiple_of(core * half, half), half)
    out[:half, :] = up[:, at]
    out[half : 2 * half, :] = down[at, :]
    mine = jnp.where(core == 0, bias[:, :half], bias[:, half:])
    row = iota((16, half), 0)
    rows = jnp.zeros((16, half), F32)
    for i, piece in enumerate(pieces(mine)):
        rows = jnp.where(row == i, piece.astype(F32), rows)
    out[2 * half :, :] = rows.astype(BF)

    model, cols = in_weights.shape[1:]
    width = heads * LANES
    row, col = (iota((cols, width), d) for d in (0, 1))
    spread = zero_one((row // HD == col // LANES) & (row % HD == col % LANES))
    lane = iota((1, width), 1) % LANES
    gap = jnp.zeros((1, HD), F32)

    def apart(line):
        return jnp.concatenate(
            sum([[line[:, h * HD : (h + 1) * HD], gap] for h in range(heads)], []), axis=1
        )

    extra = [
        apart(in_biases[0:1, :] * SCALE) + jnp.where(lane == HD, 1.0, 0.0),
        jnp.where((lane > HD) & (lane < HD + 4), 1.0, 0.0),
        apart(in_biases[1:2, :]) + jnp.where((lane >= HD) & (lane < HD + 3), 1.0, 0.0),
    ]
    for i in range(3):
        factor = SCALE if i == 0 else 1.0
        weights[:, i * width : (i + 1) * width] = (dot(in_weights[i], spread) * factor).astype(BF)
        biases[:, i * width : (i + 1) * width] = extra[i]
        for pair in range(heads // 2):
            pairs[pair, :, i * LANES : (i + 1) * LANES] = in_weights[
                i, :, pair * LANES : (pair + 1) * LANES
            ]
    tall = jnp.concatenate(
        [gains[0:1, :], shifts[0:1, :], jnp.zeros((LANES - 2, model), F32)], axis=0
    )
    columns[...] = jnp.transpose(tall)


def prepare(core, in_weights, in_biases, gains, shifts, up, down, bias, heads):
    model = up.shape[0]
    width = 3 * heads * LANES
    return local_call(
        functools.partial(prepare_kernel, heads),
        "prepare",
        (
            shaped(model, width),
            shaped(1, width, dtype=F32),
            shaped(heads // 2, model, 3 * LANES),
            shaped(model, LANES, dtype=F32),
            shaped(2 * model + 16, model),
        ),
        [SMEM] + [VMEM] * 7,
        (VMEM,) * 5,
        (core, in_weights, in_biases, gains, shifts, up, down, bias),
        cost=cost(4),
        room=ROOM,
    )


def count_of(ref, rows):
    return jnp.max(ref[rows : rows + 16, :LANES].astype(F32)).astype(jnp.int32)


def rows_at(start, rows, step=TILE):
    return pl.ds(pl.multiple_of(start, step), rows)


def attend_kernel(rows, groups, heads, *refs):
    near, far = refs[:groups], refs[groups]
    weights, biases, gains, shifts = refs[groups + 1 : groups + 5]
    at = groups + 5 + groups // 2
    out, give = refs[groups + 5 : at], refs[at]
    kept, counts, place = refs[at + 1 : at + 6], refs[at + 6], refs[at + 7]
    (xq, xk, qx, kx, vx), sems = refs[at + 8 : at + 13], refs[at + 13]
    model = xq.shape[1]
    q_counts = [count_of(r, rows) for r in near]
    k_counts = [count_of(far.at[g], rows) for g in range(groups)]
    for g in range(groups):
        counts[g] = q_counts[g]
        counts[groups + g] = k_counts[g]

    def compact(numbers, read, target):
        start = jnp.int32(0)
        for g, n in enumerate(numbers):
            target[rows_at(start, rows), :] = read(g)
            start = start + n * TILE
        target[rows_at(start, BLOCK), :] = jnp.zeros((BLOCK, model), BF)
        return start

    q_total = compact(q_counts, lambda g: near[g][:rows, :], xq)
    k_total = compact(k_counts, lambda g: far[g, :rows, :], xk)
    q_blocks = (q_total + BLOCK - 1) // BLOCK
    k_blocks = (k_total + BLOCK - 1) // BLOCK
    width = heads * LANES

    def hidden(ref, here):
        clean = standard(ref[here, :].astype(F32))[0].astype(BF)
        ref[here, :] = clean
        return (clean.astype(F32) * gains[0:1, :] + shifts[0:1, :]).astype(BF)

    @pl.loop(0, q_blocks)
    def _(b):
        here = rows_at(b * BLOCK, BLOCK, BLOCK)
        q = (dot(hidden(xq, here), weights[:, :width]) + biases[:, :width]).astype(BF)
        for h in range(heads):
            qx[h, here, :] = q[:, h * LANES : (h + 1) * LANES]

    @pl.loop(0, k_blocks)
    def _(b):
        here = rows_at(b * BLOCK, BLOCK, BLOCK)
        both = dot(hidden(xk, here), weights[:, width:]) + biases[:, width:]
        unseen = (iota((BLOCK, width), 0) + b * BLOCK >= k_total) & (
            iota((BLOCK, width), 1) % LANES == HD
        )
        k = jnp.where(unseen, FAR, both[:, :width]).astype(BF)
        v = both[:, width:].astype(BF)
        for h in range(heads):
            kx[h, here, :] = k[:, h * LANES : (h + 1) * LANES]
            vx[h, here, :] = v[:, h * LANES : (h + 1) * LANES]

    copies = [
        pltpu.make_async_copy(held, to, sems.at[i])
        for i, (held, to) in enumerate(zip((xq, xk, qx, kx, vx), kept))
    ]
    for copy in copies:
        copy.start()

    def attend_all(span):
        @pl.loop(0, q_blocks)
        def _(b):
            here = rows_at(b * BLOCK, BLOCK, BLOCK)
            lane = iota((BLOCK, LANES), 1)
            for h in range(heads):
                s = dot_nt(qx[h, here, :], kx[h, :span, :])
                top = jnp.max(s, axis=-1, keepdims=True)
                o = dot(jnp.exp(s - top).astype(BF), vx[h, :span, :])
                total = o[:, HD : HD + 1]
                o = o / total
                for i, piece in enumerate(pieces(top + jnp.log(total))):
                    o = jnp.where(lane == HD + i, piece.astype(F32), o)
                place[h, here, :] = o.astype(BF)

    for blocks in range(groups * TILE // BLOCK, groups * rows // BLOCK + 1):
        pl.when(k_blocks == blocks)(functools.partial(attend_all, blocks * BLOCK))

    gather = [
        (iota((LANES, LANES), 0) - HD + 3 * h == iota((LANES, LANES), 1))
        & (iota((LANES, LANES), 0) >= HD)
        & (iota((LANES, LANES), 0) < HD + 3)
        for h in range(heads)
    ]
    gather = [jnp.where(m, 1.0, 0.0).astype(BF) for m in gather]
    start = jnp.int32(0)
    for g in range(groups):
        mine = [place[h, rows_at(start, rows), :] for h in range(heads)]
        stats = sum(dot(m, s) for m, s in zip(mine, gather)).astype(BF)
        value = jnp.concatenate([m[:, :HD] for m in mine] + [stats], axis=1)
        if g < groups // 2:
            out[g][...] = value
        else:
            give[g - groups // 2] = value
        start = start + q_counts[g] * TILE
    for copy in copies:
        copy.wait()


def attend(near, far, weights, biases, gains, shifts, rows, heads):
    groups = len(near)
    model = near[0].shape[1]
    room = rows * groups + BLOCK
    parts = heads * HD + LANES
    kept = [(room, model)] * 2 + [(heads, room, LANES)] * 3
    return local_call(
        functools.partial(attend_kernel, rows, groups, heads),
        "attend",
        (
            *[shaped(rows, parts)] * (groups // 2),
            shaped(groups // 2, rows, parts),
            *[shaped(*k) for k in kept],
            shaped(2 * groups, dtype=jnp.int32),
        ),
        [VMEM] * (groups + 5),
        (*[VMEM] * (groups // 2 + 1), *[ANY] * 5, SMEM),
        (*near, far, weights, biases, gains, shifts),
        [
            pltpu.VMEM((heads, room, LANES), BF),
            *[pltpu.VMEM(k, BF) for k in kept],
            pltpu.SemaphoreType.DMA((5,)),
        ],
        cost(15),
        ROOM,
    )


def same_tile(rows):
    return iota((rows, rows), 0) // TILE == iota((rows, rows), 1) // TILE


def thumb_kernel(heads, tokens, weights, biases, gains, shifts, out, xhat, x):
    width = heads * LANES
    size = tokens.shape[0]
    clean = standard(tokens[...].astype(F32))[0].astype(BF)
    xhat[...] = clean
    hidden = (clean.astype(F32) * gains[0:1, :] + shifts[0:1, :]).astype(BF)
    x[...] = (dot(hidden, weights[...]) + biases[...]).astype(BF)
    visible = same_tile(size - TILE)
    out[:TILE, :] = jnp.zeros((TILE, heads * HD), F32)
    for h in range(heads):
        q = x[TILE:, h * LANES : (h + 1) * LANES]
        k = x[TILE:, width + h * LANES : width + (h + 1) * LANES]
        v = x[TILE:, 2 * width + h * LANES : 2 * width + (h + 1) * LANES]
        s = jnp.where(visible, dot_nt(q, k), FAR)
        e = jnp.exp(s - jnp.max(s, axis=-1, keepdims=True))
        o = dot(e.astype(BF), v)[:, :HD] / jnp.sum(e, axis=-1, keepdims=True)
        out[TILE:, h * HD : (h + 1) * HD] = o


def thumbs(tokens, weights, biases, gains, shifts, heads):
    size, model = tokens.shape
    return local_call(
        functools.partial(thumb_kernel, heads),
        "thumbs",
        (
            shaped(size, heads * HD, dtype=F32),
            shaped(size, model),
            shaped(size, 3 * heads * LANES),
        ),
        [VMEM] * 5,
        (VMEM,) * 3,
        (tokens, weights, biases, gains, shifts),
        cost=cost(5),
    )


def merged(parts, heads):
    cols = heads * HD
    row, col = (iota((LANES, cols), d) for d in (0, 1))
    spread = zero_one(row // 3 == col // HD)
    marks = [dot(p[:, cols:], spread) for p in parts]
    top = functools.reduce(jnp.maximum, marks)
    expos = [jnp.exp(m - top) for m in marks]
    total = sum(expos)
    mixed = sum(e * p[:, :cols].astype(F32) for p, e in zip(parts, expos)) / total
    row, col = (iota((cols, LANES), d) for d in (0, 1))
    packed = [
        dot(piece, zero_one((row % HD == 0) & (col == 3 * (row // HD) + i)))
        for i, piece in enumerate(pieces(top + jnp.log(total)))
    ]
    return mixed, sum(packed)


def pair_kernel(heads, *refs):
    count = (len(refs) - 1) // 2
    for j, (mine, out) in enumerate(zip(refs[:count], refs[count + 1 :])):
        mixed, marks = merged([mine[...], refs[count][j]], heads)
        out[...] = jnp.concatenate([mixed.astype(BF), marks.astype(BF)], axis=1)


def pair_merge(parts, other, heads):
    return local_call(
        functools.partial(pair_kernel, heads),
        "pair_merge",
        tuple(shaped(*p.shape) for p in parts),
        [VMEM] * (len(parts) + 1),
        (VMEM,) * len(parts),
        (*parts, other),
        cost=cost(3),
        room=ROOM,
    )


def merge_kernel(heads, counts, thumb, *refs):
    parts, (low, full, lse) = refs[:-3], refs[-3:]
    cols = heads * HD
    rows = lse.shape[0]
    mixed, marks = merged([p[...] for p in parts], heads)
    lse[...] = (-marks).astype(BF)
    image = iota((rows, cols), 0) < counts[0] * TILE
    full[:rows, :] = jnp.where(image, mixed, thumb[:rows, :])
    full[rows:, :] = thumb[rows:, :]
    low[...] = full[...].astype(BF)


def merge(count, parts, thumb, heads):
    size, cols = thumb.shape
    return local_call(
        functools.partial(merge_kernel, heads),
        "merge",
        (shaped(size, cols), shaped(size, cols, dtype=F32), shaped(parts[0].shape[0], LANES)),
        [SMEM] + [VMEM] * (1 + len(parts)),
        (VMEM,) * 3,
        (count, thumb, *parts),
        cost=cost(3),
    )


def fold_kernel(*refs):
    count = (len(refs) - 1) // 2
    for j, (mine, out) in enumerate(zip(refs[:count], refs[count + 1 :])):
        out[...] = (mine[...].astype(F32) + refs[count][j].astype(F32)).astype(BF)


def fold(parts, other):
    return local_call(
        fold_kernel,
        "fold",
        tuple(shaped(*p.shape) for p in parts),
        [VMEM] * (len(parts) + 1),
        (VMEM,) * len(parts),
        (*parts, other),
        cost=cost(2),
        room=ROOM,
    )


ROOT = 0.7978845608028654
CUBE = 0.044715


def ff_kernel(
    heads, tokens, outer, low, low_far, full, lse, out_weight, out_far, up, up_bias, down, far_one,
    far_two, gains, shifts, mixed, grad_mid, grad_low, packed, hidden_out, act_out, pre_out, small,
):
    size, model = tokens.shape
    passes = outer.shape[0]
    cols = heads * HD
    chunk = far_one.shape[1]
    units = up.shape[1]
    rows = packed.shape[0]
    branch = dot(low[...], out_weight[...]) + dot(low_far[...], out_far[...])
    middle = tokens[...].astype(F32) + (branch + shifts[1:2, :])
    xhat, factor = standard(middle)
    hidden = (xhat * gains[1:2, :] + shifts[2:3, :]).astype(BF)
    hidden_out[...] = hidden

    def one_chunk(up_part, bias, down_part, keep):
        v = dot(hidden, up_part) + bias
        t = jnp.tanh(ROOT * (v + CUBE * (v * v * v)))
        act = (0.5 * v * (1.0 + t)).astype(BF)
        slope = 0.5 * (1.0 + t) + 0.5 * v * (1.0 - t * t) * (ROOT * (1.0 + 3.0 * CUBE * (v * v)))
        two = []
        for p in range(passes):
            pre = (dot_nt(outer[p], down_part) * slope).astype(BF)
            if keep is not None:
                pre_out[p, :, keep] = pre
            two.append(dot_nt(pre, up_part))
        if keep is not None:
            act_out[:, keep] = act
        return dot(act, down_part), two

    def far_chunk(ref):
        told = ref[2 * chunk : 2 * chunk + 16, :].astype(F32)
        bias = told[0:1] + told[1:2] + told[2:3]
        return one_chunk(ref[:chunk, :], bias, ref[chunk : 2 * chunk, :], None)

    done = []
    for i in range(units // chunk):
        at = slice(i * chunk, (i + 1) * chunk)
        done.append(one_chunk(up[:, at], up_bias[:, at], down[at, :], at))
    done += [far_chunk(far_one), far_chunk(far_two)]

    def tree(parts):
        half = len(parts) // 2
        return sum(parts[:half]) + sum(parts[half:])

    output = tree([d[0] for d in done])
    mixed[...] = (middle + (output + shifts[3:4, :])).astype(BF)
    small[...] = jnp.zeros(small.shape, F32)
    lane = iota((rows, LANES), 1)
    stats = jnp.zeros((rows, LANES), F32)
    for p in range(passes):
        two = tree([d[1][p] for d in done])
        c = outer[p].astype(F32)
        mid = c + norm_back(two, gains[1:2, :], xhat, factor)
        mid_low = mid.astype(BF)
        grad_mid[p] = mid
        grad_low[p] = mid_low
        att = dot_nt(mid_low, out_weight[...]).astype(BF)
        packed[:, p * cols : (p + 1) * cols] = att[:rows, :]
        pre_out_p = pre_out[p].astype(F32)
        bias = jnp.sum(pre_out_p, axis=0, keepdims=True)
        small[p, 0:1, :] = jnp.sum(two * xhat, axis=0, keepdims=True)
        small[p, 1:2, :] = jnp.sum(two, axis=0, keepdims=True)
        small[p, 2:3, :] = jnp.sum(mid_low.astype(F32), axis=0, keepdims=True)
        small[p, 3:4, :] = jnp.sum(c, axis=0, keepdims=True)
        for i in range(units // model):
            small[p, 4 + i : 5 + i, :] = bias[:, i * model : (i + 1) * model]
        product = att[:rows, :].astype(F32) * full[:rows, :]
        for h in range(heads):
            delta = jnp.sum(product[:, h * HD : (h + 1) * HD], axis=-1, keepdims=True)
            for i, piece in enumerate(pieces(-delta)):
                stats = jnp.where(lane == 3 * heads * (p + 1) + 3 * h + i, piece.astype(F32), stats)
    packed[:, passes * cols :] = (stats + lse[...].astype(F32)).astype(BF)


def feed_forward(
    tokens, outer, low, low_far, full, lse, out_weight, out_far, up, up_bias, down, far_one, far_two,
    gains, shifts, rows, heads,
):
    size, model = tokens.shape
    passes = outer.shape[0]
    units = up.shape[1]
    return local_call(
        functools.partial(ff_kernel, heads),
        "feed_forward",
        (
            shaped(size, model),
            shaped(passes, size, model, dtype=F32),
            shaped(passes, size, model),
            shaped(rows, passes * heads * HD + LANES),
            shaped(size, model),
            shaped(size, units),
            shaped(passes, size, units),
            shaped(passes, 8, model, dtype=F32),
        ),
        [VMEM] * 15,
        (VMEM,) * 8,
        (
            tokens, outer, low, low_far, full, lse, out_weight, out_far, up, up_bias, down, far_one,
            far_two, gains, shifts,
        ),
        cost=cost(12),
        room=32,
    )


def thumb_back_kernel(heads, counts, x, mid_low, out_weight, out):
    width = heads * LANES
    size = x.shape[0]
    passes = mid_low.shape[0]
    visible = same_tile(size - TILE)
    outside = iota((size - TILE, HD), 0) + TILE >= counts[0] * TILE
    grads = [dot_nt(mid_low[p], out_weight[...]).astype(BF) for p in range(passes)]
    out[:, :, :TILE, :] = jnp.zeros((*out.shape[:2], TILE, out.shape[3]), BF)
    for h in range(heads):
        q = x[TILE:, h * LANES : (h + 1) * LANES]
        k = x[TILE:, width + h * LANES : width + (h + 1) * LANES]
        v = x[TILE:, 2 * width + h * LANES : 2 * width + h * LANES + HD]
        s = jnp.where(visible, dot_nt(q, k), FAR)
        e = jnp.exp(s - jnp.max(s, axis=-1, keepdims=True))
        w = e / jnp.sum(e, axis=-1, keepdims=True)
        w_low = w.astype(BF)
        for p in range(passes):
            g = grads[p][TILE:, h * HD : (h + 1) * HD]
            gw = dot_nt(g, v)
            ds = (w * (gw - jnp.sum(w * gw, axis=-1, keepdims=True))).astype(BF)
            dq = dot(ds, k[:, :HD]) * SCALE
            dk = dot_tn(ds, q)[:, :HD]
            dv = dot_tn(w_low, g)
            for c, piece in enumerate((dq, dk, dv)):
                at = c * LANES + (h % 2) * HD
                out[h // 2, p, TILE:, at : at + HD] = jnp.where(outside, piece, 0.0).astype(BF)


def thumbs_back(count, x, mid_low, out_weight, heads):
    passes, size, _ = mid_low.shape
    return local_call(
        functools.partial(thumb_back_kernel, heads),
        "thumbs_back",
        shaped(heads // 2, passes, size, 3 * LANES),
        [SMEM] + [VMEM] * 3,
        VMEM,
        (count, x, mid_low, out_weight),
        cost=cost(6),
    )


def early_at(units, model, low):
    ends = [model, 2 * model, 2 * model + units, 2 * model + units + low]
    return [slice(b - w, b) for b, w in zip(ends, (model, model, units, low))]


def early_cuts(parts, units, model, low):
    high, wide, turns = units // parts // 2, model // parts, model // low
    narrow = low * turns // parts
    for i in range(parts):
        yield (
            (slice(2 * i * high, (2 * i + 1) * high), slice(0, model)),
            (slice((2 * i + 1) * high, (2 * i + 2) * high), slice(0, model)),
            (slice(i * wide, (i + 1) * wide), slice(0, units)),
            (
                slice(i // turns * narrow, (i // turns + 1) * narrow),
                slice(i % turns * low, (i % turns + 1) * low),
            ),
        )


def weight_kernel(place, act, outer, hidden, pre, low, mid_low, keep, give):
    units, model, cols = act.shape[1], hidden.shape[1], low.shape[1]
    core = place[0]
    for turn, out in ((core, keep), (1 - core, give)):
        down = dot_tn(act[...], outer[turn]).astype(BF)
        up = dot_tn(hidden[...], pre[turn]).astype(BF)
        proj = dot_tn(low[...], mid_low[turn]).astype(BF)
        for i, cut in enumerate(early_cuts(keep.shape[0], units, model, cols)):
            for value, (rows, lanes), at in zip(
                (down, down, up, proj), cut, early_at(units, model, cols)
            ):
                out[i, :, at] = value[rows, lanes]


def weight_grads(core, act, outer, hidden, pre, low, mid_low, parts):
    units, model = act.shape[1], outer.shape[2]
    out = shaped(parts, model // parts, 2 * model + units + low.shape[1])
    return local_call(
        weight_kernel,
        "weight_grads",
        (out, out),
        [SMEM] + [VMEM] * 6,
        (VMEM,) * 2,
        (core, act, outer, hidden, pre, low, mid_low),
        cost=cost(8),
        room=24,
    )


def reverse_kernel(rows, groups, heads, passes, counts, place, *refs):
    grads, kept = refs[:groups], refs[groups : groups + 5]
    own, thumb, weights, columns, small = refs[groups + 5 : groups + 10]
    at = groups + 10
    out_q, give_q, at = refs[at : at + groups // 2], refs[at + groups // 2], at + groups // 2 + 1
    out_kv, at = refs[at : at + groups // 2], at + groups // 2
    keep, give = refs[at : at + 2]
    (
        stage, xq, xk, qx, kx, vx, packed, gx, kt, dq_t, dv, dk, low_q, low_kv, total, sums,
        starts, sems,
    ) = refs[at + 2 :]
    couples = heads // 2
    sources = [*grads, *kept[2:], *kept[:2]]
    targets = [*[stage.at[g] for g in range(groups)], qx, kx, vx, xq, xk]
    copies = [
        pltpu.make_async_copy(f, t, sems.at[i]) for i, (f, t) in enumerate(zip(sources, targets))
    ]
    for copy in copies:
        copy.start()
    cols = heads * HD
    wide = passes * LANES
    q_counts = [counts[g] for g in range(groups)]
    k_counts = [counts[groups + g] for g in range(groups)]
    start = jnp.int32(0)
    for g in range(groups):
        copies[g].wait()
        packed[rows_at(start, rows), :] = stage[g]
        start = start + q_counts[g] * TILE
    q_total, k_total = start, sum(k_counts) * TILE
    tail_lane = iota((BLOCK, packed.shape[1]), 1) - passes * cols
    empty = (tail_lane >= 0) & (tail_lane < 3 * heads) & (tail_lane % 3 == 0)
    packed[rows_at(q_total, BLOCK), :] = jnp.where(empty, FAR, 0.0).astype(BF)
    q_blocks = (q_total + BLOCK - 1) // BLOCK
    k_blocks = (k_total + BLOCK - 1) // BLOCK
    spans = range(groups * TILE // BLOCK, groups * rows // BLOCK + 1)

    row, col = (iota((LANES, heads * LANES), d) for d in (0, 1))
    head, lane = col // LANES, col % LANES
    to_marks = zero_one((lane > HD) & (lane < HD + 4) & (row == 3 * head + lane - HD - 1))
    row, col = (iota((LANES, heads * wide), d) for d in (0, 1))
    head, turn, lane = col // wide, col % wide // LANES, col % LANES
    to_deltas = zero_one(
        (lane >= HD) & (lane < HD + 3) & (row == 3 * heads * (turn + 1) + 3 * head + lane - HD)
    )
    for copy in copies[groups : groups + 3]:
        copy.wait()

    @pl.loop(0, q_blocks)
    def _(b):
        here = rows_at(b * BLOCK, BLOCK, BLOCK)
        stats = packed[here, passes * cols :]
        marks = dot(stats, to_marks)
        deltas = dot(stats, to_deltas).astype(BF)
        for h in range(heads):
            more = marks[:, h * LANES : (h + 1) * LANES]
            qx[h, here, :] = (qx[h, here, :].astype(F32) + more).astype(BF)
            for p in range(passes):
                at = p * cols + h * HD
                mine = (h * passes + p) * LANES
                gx[h, here, p * LANES : (p + 1) * LANES] = jnp.concatenate(
                    [packed[here, at : at + HD], deltas[:, mine + HD : mine + LANES]], axis=1
                )

    @pl.loop(0, k_blocks)
    def _(b):
        here = rows_at(b * BLOCK, BLOCK, BLOCK)
        for h in range(heads):
            kt[h, b] = jnp.transpose(kx[h, here, :].astype(F32))[:HD, :].astype(BF)

    def reverse_all(blocks):
        span = blocks * BLOCK

        @pl.loop(0, couples)
        def _(pair):
            dv[:, :span, :] = jnp.zeros((2, span, wide), F32)
            dk[:, :, :span, :] = jnp.zeros((passes, 2, span, LANES), F32)

            @pl.loop(0, q_blocks)
            def _(b):
                here = rows_at(b * BLOCK, BLOCK, BLOCK)
                for i in range(2):
                    h = 2 * pair + i
                    q, g = qx[h, here, :], gx[h, here, :]
                    k_t = jnp.concatenate([kt[h, j] for j in range(blocks)], axis=1)
                    w = jnp.exp(dot_nt(kx[h, :span, :], q))
                    dv[i, :span, :] += dot(w.astype(BF), g)
                    for p in range(passes):
                        ds = dot_nt(vx[h, :span, :], g[:, p * LANES : (p + 1) * LANES])
                        ds = (w * ds).astype(BF)
                        dk[p, i, :span, :] += dot(ds, q)
                        dq_t[p, i * HD : (i + 1) * HD, :] = dot(k_t, ds)
                for p in range(passes):
                    piece = jnp.transpose(dq_t[p]) * SCALE
                    low_q[pair, here, p * LANES : (p + 1) * LANES] = piece.astype(BF)

            for p in range(passes):
                for c, both in enumerate(
                    (
                        [dk[p, i, :span, :HD] for i in range(2)],
                        [dv[i, :span, p * LANES : p * LANES + HD] for i in range(2)],
                    )
                ):
                    lane = (2 * p + c) * LANES
                    low_kv[pair, :span, lane : lane + LANES] = jnp.concatenate(both, axis=1).astype(BF)

    for blocks in spans:
        pl.when(k_blocks == blocks)(functools.partial(reverse_all, blocks))

    start = jnp.int32(0)
    for g in range(groups):
        starts[g] = start
        start = start + k_counts[g] * TILE
    for g in range(groups):
        here = rows_at(starts[place[1 + g]], rows)
        out_kv[g // 2][g % 2] = jnp.concatenate([low_kv[i, here, :] for i in range(couples)], axis=1)
    start = jnp.int32(0)
    for g in range(groups):
        here = rows_at(start, rows)
        value = jnp.concatenate([low_q[i, here, :] for i in range(couples)], axis=1)
        if g < groups // 2:
            out_q[g][...] = value
        else:
            give_q[g - groups // 2] = value
        start = start + q_counts[g] * TILE

    copies[groups + 3].wait()
    copies[groups + 4].wait()

    def key_sums(blocks):
        span = blocks * BLOCK
        for i in range(couples):
            flat = low_kv[i, :span, :]
            total[i, :, wide:] = dot_tn(xk[:span, :], flat)
            sums[i, :, wide:] = dot(jnp.ones((8, span), BF), flat)

    for blocks in spans:
        pl.when(k_blocks == blocks)(functools.partial(key_sums, blocks))

    total[:, :, :wide] = jnp.zeros((couples, total.shape[1], wide), F32)
    sums[:, :, :wide] = jnp.zeros((couples, 8, wide), F32)

    @pl.loop(0, q_blocks)
    def _(b):
        here = rows_at(b * BLOCK, BLOCK, BLOCK)
        for i in range(couples):
            total[i, :, :wide] += dot_tn(xq[here, :], low_q[i, here, :])
            sums[i, :, :wide] += dot(jnp.ones((8, BLOCK), BF), low_q[i, here, :])

    model = total.shape[1]
    gain, shift = columns[:, 0:1], columns[:, 1:2]
    ones = jnp.ones((8, own.shape[0]), BF)
    for p in range(passes):
        whole = []
        for i in range(couples):
            mine = thumb[i, p]
            part = dot_tn(own[...], mine)
            part_sum = dot(ones, mine)[0:1, :]
            q_at = slice(p * LANES, (p + 1) * LANES)
            kv_at = slice((passes + 2 * p) * LANES, (passes + 2 * p + 2) * LANES)
            part += jnp.concatenate([total[i, :, q_at], total[i, :, kv_at]], axis=1)
            part_sum += jnp.concatenate([sums[i, 0:1, q_at], sums[i, 0:1, kv_at]], axis=1)
            w = weights[i].astype(F32)
            gain_one = jnp.sum(w * part, axis=1, keepdims=True)
            shift_one = jnp.sum(w * part_sum, axis=1, keepdims=True)
            lane = iota((model, LANES), 1)
            tall = jnp.where(lane == 0, gain_one, jnp.where(lane == 1, shift_one, 0.0))
            flat = jnp.concatenate(
                [jnp.zeros((2, LANES), F32)]
                + [part_sum[:, c * LANES : (c + 1) * LANES] for c in range(3)]
                + [jnp.zeros((LANES - 5, LANES), F32)],
                axis=0,
            )
            tall = jnp.concatenate([tall[:LANES] + jnp.transpose(flat), tall[LANES:]], axis=0)
            if i == 0:
                turned = jnp.concatenate(
                    [
                        jnp.zeros((8, model), F32),
                        small[p],
                        jnp.zeros((LANES - 16, model), F32),
                    ],
                    axis=0,
                )
                tall = tall + jnp.transpose(turned)
            whole += [part * gain + shift * part_sum, tall]
        whole = jnp.concatenate(whole, axis=1).astype(BF)

        @pl.when(place[0] == p)
        def _():
            keep[...] = whole

        @pl.when(place[0] != p)
        def _():
            give[...] = whole


def reverse(counts, place, grads, kept, own, thumb, weights, columns, small, rows, heads):
    groups = len(grads)
    couples, passes = thumb.shape[:2]
    model = own.shape[1]
    room = rows * groups + BLOCK
    cols = heads * HD
    wide = passes * LANES
    half = groups // 2
    late = shaped(model, couples * 4 * LANES)
    q, kv = shaped(rows, couples * wide), shaped(2, rows, couples * 2 * wide)
    out = (*[q] * half, shaped(half, rows, couples * wide), *[kv] * half, late, late)
    return local_call(
        functools.partial(reverse_kernel, rows, groups, heads, passes),
        "reverse",
        out,
        [SMEM, SMEM] + [ANY] * (groups + 5) + [VMEM] * 5,
        (VMEM,) * len(out),
        (counts, place, *grads, *kept, own, thumb, weights, columns, small),
        [
            pltpu.VMEM((groups, rows, passes * cols + LANES), BF),
            pltpu.VMEM((room, model), BF),
            pltpu.VMEM((room, model), BF),
            pltpu.VMEM((heads, room, LANES), BF),
            pltpu.VMEM((heads, room, LANES), BF),
            pltpu.VMEM((heads, room, LANES), BF),
            pltpu.VMEM((room, passes * cols + LANES), BF),
            pltpu.VMEM((heads, room, wide), BF),
            pltpu.VMEM((heads, room // BLOCK, HD, BLOCK), BF),
            pltpu.VMEM((passes, LANES, BLOCK), F32),
            pltpu.VMEM((2, room, wide), F32),
            pltpu.VMEM((passes, 2, room, LANES), F32),
            pltpu.VMEM((couples, room, wide), BF),
            pltpu.VMEM((couples, room, 2 * wide), BF),
            pltpu.VMEM((couples, model, 3 * wide), F32),
            pltpu.VMEM((couples, 8, 3 * wide), F32),
            pltpu.SMEM((groups,), jnp.int32),
            pltpu.SemaphoreType.DMA((groups + 5,)),
        ],
        cost(45),
        ROOM,
    )


def grad_one_kernel(near, counts, *refs):
    from_q, from_kv, (thumb, weights, mine, other) = refs[:near], refs[near:-4], refs[-4:]
    couples, passes, size, _ = thumb.shape
    rows = from_q[0].shape[0]
    sum_q = sum(r[...].astype(F32) for r in from_q)
    sum_kv = [sum(r[f].astype(F32) for r in from_kv) for f in range(2)]
    image = iota((rows, 3 * LANES), 0) < counts[0] * TILE
    for p in range(passes):
        parts = []
        for i in range(couples):
            at = (passes * i + p) * LANES
            there = slice(2 * at, 2 * at + 2 * LANES)
            far = jnp.concatenate([sum_q[:, at : at + LANES], sum_kv[0][:, there]], axis=1)
            flat = jnp.concatenate(
                [jnp.where(image, far.astype(BF), thumb[i, p, :rows]), thumb[i, p, rows:]], axis=0
            )
            parts.append(
                (
                    dot_nt(flat, weights[i]),
                    dot_nt(sum_kv[1][:, there].astype(BF), weights[i, :, LANES:]),
                )
            )
        mine[p] = sum(a for a, _ in parts).astype(BF)
        other[p] = sum(b for _, b in parts).astype(BF)


def grad_one(count, from_q, from_kv, thumb, weights):
    near = len(from_q)
    passes, size, _ = thumb.shape[1:]
    model = weights.shape[1]
    return local_call(
        functools.partial(grad_one_kernel, near),
        "grad_one",
        (shaped(passes, size, model), shaped(passes, from_q[0].shape[0], model)),
        [SMEM] + [VMEM] * (near + len(from_kv) + 2),
        (VMEM,) * 2,
        (count, *from_q, *from_kv, thumb, weights),
        cost=cost(5),
        room=ROOM,
    )


def close_kernel(counts, tokens, mid, mine, head, side, cross, gains, out):
    xhat, factor = standard(tokens[...].astype(F32))
    rows = side.shape[1]
    image = iota(side.shape[1:], 0) < counts[0] * TILE
    for p in range(mid.shape[0]):
        grad = mine[p].astype(F32) + head[p].astype(F32)
        more = jnp.where(image, side[p].astype(F32) + cross[p].astype(F32), 0.0)
        grad = jnp.concatenate([grad[:rows] + more, grad[rows:]], axis=0)
        out[p] = mid[p] + norm_back(grad, gains[0:1, :], xhat, factor)


def close(count, tokens, mid, mine, head, side, cross, gains):
    return local_call(
        close_kernel,
        "close",
        shaped(*mid.shape, dtype=F32),
        [SMEM] + [VMEM] * 7,
        VMEM,
        (count, tokens, mid, mine, head, side, cross, gains),
        cost=cost(4),
        room=ROOM,
    )


def early_kernel(lines, far, place, *refs):
    parts, refs = refs[:lines], refs[lines:]
    out, (down, up, proj, sems) = refs[-7:-4], refs[-4:]
    turn, y = place[0], place[10]
    turn = 1 - turn if far else turn
    (units, model), low = down.shape, proj.shape[0]
    steps, rows = parts[0].shape[:2]
    lane_down, lane_next, lane_up, lane_proj = early_at(units, model, low)
    turns = model // low
    for d, ref in enumerate(parts):
        for j in range(steps):
            i = j * lines + (y + lines - d) % lines
            at = pl.multiple_of(2 * rows * i, 2 * rows)
            down[pl.ds(at, rows), :] = ref[j, :, lane_down].astype(F32)
            down[pl.ds(at + rows, rows), :] = ref[j, :, lane_next].astype(F32)
            up[rows_at(rows * i, rows, rows), :] = ref[j, :, lane_up].astype(F32)
            here = rows_at(i // turns * rows, rows, rows)
            value = ref[j, :, lane_proj].astype(F32)
            for t in range(turns):

                @pl.when(i % turns == t)
                def _(value=value, here=here, t=t):
                    proj[here, t * low : (t + 1) * low] = value

    copies = [
        pltpu.make_async_copy(held, to.at[turn], sems.at[n])
        for n, (held, to) in enumerate(zip((down, up, proj), out))
    ]
    for copy in copies:
        copy.start()
    for copy in copies:
        copy.wait()


def early_out(place, parts, before, units, low):
    model = len(parts) * parts[0].shape[0] * parts[0].shape[1]
    shapes = (units, model), (model, units), (low, model)
    return pl.pallas_call(
        functools.partial(early_kernel, len(parts), bool(before)),
        out_shape=tuple(shaped(2, *s, dtype=F32) for s in shapes),
        in_specs=[SMEM] + [VMEM] * len(parts) + [ANY] * len(before),
        out_specs=(ANY,) * 3,
        scratch_shapes=[
            *[pltpu.VMEM(s, F32) for s in shapes],
            pltpu.SemaphoreType.DMA((3,)),
        ],
        input_output_aliases={1 + len(parts) + i: i for i in range(len(before))},
        cost_estimate=cost(5),
        compiler_params=pltpu.CompilerParams(vmem_limit_bytes=ROOM * MIB),
        name="early_far" if before else "early_own",
    )(place, *parts, *before)


def late_kernel(far, place, ref, *refs):
    out, (grad_in, *small), sems = refs[-11:-6], refs[-6:-1], refs[-1]
    in_bias, up_bias, gains, shifts = small
    turn = 1 - place[0] if far else place[0]
    turned = []
    for pair in range(2):
        at = 4 * LANES * pair
        for c in range(3):
            grad_in[c, :, pair * LANES : (pair + 1) * LANES] = ref[
                :, at + c * LANES : at + (c + 1) * LANES
            ].astype(F32)
        turned.append(jnp.transpose(ref[:, at + 3 * LANES : at + 4 * LANES].astype(F32)))
    a, b = turned
    in_bias[...] = jnp.concatenate(
        [
            jnp.concatenate([a[2:3, :LANES], b[2:3, :LANES]], axis=1),
            jnp.concatenate([a[4:5, :LANES], b[4:5, :LANES]], axis=1),
        ],
        axis=0,
    )
    up_bias[...] = jnp.concatenate([a[12:13], a[13:14]], axis=1)
    gains[...] = jnp.concatenate([a[0:1] + b[0:1], a[8:9]], axis=0)
    shifts[...] = jnp.concatenate([a[1:2] + b[1:2], a[10:11], a[9:10], a[11:12]], axis=0)
    copies = [
        pltpu.make_async_copy(held, to.at[turn], sems.at[n])
        for n, (held, to) in enumerate(zip((grad_in, *small), out))
    ]
    for copy in copies:
        copy.start()
    for copy in copies:
        copy.wait()


def late_out(place, part, before, units):
    model = part.shape[0]
    shapes = (3, model, 2 * LANES), (2, 2 * LANES), (1, units), (2, model), (4, model)
    return pl.pallas_call(
        functools.partial(late_kernel, bool(before)),
        out_shape=tuple(shaped(2, *s, dtype=F32) for s in shapes),
        in_specs=[SMEM, VMEM] + [ANY] * len(before),
        out_specs=(ANY,) * 5,
        scratch_shapes=[
            *[pltpu.VMEM(s, F32) for s in shapes],
            pltpu.SemaphoreType.DMA((5,)),
        ],
        input_output_aliases={2 + i: i for i in range(len(before))},
        cost_estimate=cost(3),
        compiler_params=pltpu.CompilerParams(vmem_limit_bytes=ROOM * MIB),
        name="late_far" if before else "late_own",
    )(place, part, *before)


def gather_near(array):
    mine = [array] + [shift_by(array, "y", d) for d in range(1, lax.axis_size("y"))]
    return mine + [shift_by(a, "c", 1) for a in mine]


def return_near(parts):
    return [parts[0]] + [shift_by(p, "y", -j) for j, p in enumerate(parts) if j > 0]


def offsets(size):
    return [(step, flip) for step in range(size) for flip in range(2)]


def return_far(parts):
    return [parts[0]] + [shift_by(p, "z", step) for step, p in enumerate(parts) if step > 0]


PLANE = ("z", "y")


def core_sum(keep, give):
    return (keep.astype(F32) + shift_by(give, "c", 1).astype(F32)).astype(BF)


def crossed(array):
    n = lax.axis_size(("xl", "h"))
    return lax.ppermute(array, ("xl", "h"), [(i, n - 1 - i) for i in range(n)])


def across(low):
    done = low.astype(F32) + shift_by(low, "xl", 1).astype(F32)
    size = 4 * LANES
    ones = jnp.concatenate([low[:, i + 3 * LANES : i + size] for i in range(0, low.shape[1], size)], axis=1)
    more = shift_by(ones, "h", 1).astype(F32) + crossed(ones).astype(F32)
    more = jnp.where(jnp.arange(more.shape[1]) % LANES < 2, more, 0.0)
    nothing = jnp.zeros((low.shape[0], 3 * LANES), F32)
    laid = [[nothing, more[:, i : i + LANES]] for i in range(0, more.shape[1], LANES)]
    return (done + jnp.concatenate(sum(laid, []), axis=1)).astype(BF)


def tied(arrays, others):
    return lax.optimization_barrier((arrays, others))


def local(
    tokens,
    cotangents,
    segment_ids,
    in_weights,
    in_biases,
    out_weight,
    up_weight,
    up_biases,
    down_weight,
    gains,
    shifts,
):
    size, model = tokens.shape
    cols = in_weights.shape[2]
    heads = cols // HD
    rows = size - TILE
    units = up_weight.shape[1]
    c = lax.axis_index("c")

    told, copies, count = front(tokens, segment_ids, lax.axis_size(("z", "xl")))
    far = lax.all_to_all(copies, ("z", "xl"), 0, 0, tiled=True)
    near = gather_near(told)
    core = c.astype(jnp.int32).reshape(1)
    z, xl, z_size = lax.axis_index("z"), lax.axis_index("xl"), lax.axis_size("z")
    routes = [((z + step) % z_size) * 2 + (xl ^ flip) for step, flip in offsets(z_size)]
    place = jnp.stack([c, *routes, z, lax.axis_index("y")]).astype(jnp.int32)
    plane = lax.axis_size(PLANE)

    weights, biases, pairs, columns, bundle = prepare(
        core, in_weights, in_biases, gains, shifts, up_weight, down_weight, up_biases[None], heads
    )
    out_far = crossed(out_weight)
    far_one = crossed(bundle)
    far_two = shift_by(far_one, "c", 1)

    weights, (out_far, columns, place) = tied(weights, (out_far, columns, place))
    *parts, give, xq, xk, qx, kx, vx, counts = attend(
        near, far, weights, biases, gains, shifts, rows, heads
    )
    thumb_out, xhat, x = thumbs(tokens, weights, biases, gains, shifts, heads)
    parts = pair_merge(parts, shift_by(give, "c", 1), heads)
    low, full, lse = merge(count, return_near(parts), thumb_out, heads)
    low_far = shift_by(low, "h", 1)
    mixed, grad_mid, mid_low, packed, hidden, act, pre, small = feed_forward(
        tokens, cotangents, low, low_far, full, lse, out_weight, out_far, up_weight, up_biases[None],
        down_weight, far_one, far_two, gains, shifts, rows, heads,
    )
    grads = gather_near(packed)
    keep, give = weight_grads(core, act, cotangents, hidden, pre, low, mid_low, plane)
    mid_low, (keep, give) = tied(mid_low, (keep, give))
    thumb = thumbs_back(count, x, mid_low, out_weight, heads)
    early = core_sum(keep, give)

    grads, (early, thumb) = tied(grads, (early, thumb))
    early = lax.all_to_all(early, PLANE, 0, 0, tiled=True)
    *out, keep, give = reverse(
        counts, place, grads, (xq, xk, qx, kx, vx), xhat, thumb, pairs, columns, small, rows, heads
    )
    half = len(near) // 2
    out_q, give_q, out_kv = out[:half], out[half], out[half + 1 :]
    early = jnp.sum(early.astype(F32), axis=0).astype(BF)
    early = (early.astype(F32) + shift_by(early, "xl", 1).astype(F32)).astype(BF)
    early = jnp.broadcast_to(early[None], (z_size, *early.shape))
    late, early = tied(core_sum(keep, give), early)
    early = lax.all_to_all(early, "z", 0, 0, tiled=True)
    from_kv = return_far(out_kv)
    out_q = fold(out_q, shift_by(give_q, "c", 1))
    from_q = return_near(out_q)
    late, (early, from_kv[1], from_kv[-1], from_q) = tied(
        late, (early, from_kv[1], from_kv[-1], from_q)
    )
    late = late.reshape(plane, -1, late.shape[1])
    late = lax.all_to_all(late, PLANE, 0, 0, tiled=True)
    early = [early] + [shift_by(early, "y", d) for d in range(1, lax.axis_size("y"))]
    mine, other = grad_one(count, from_q, from_kv, thumb, pairs)
    late, (early[1], early[-1]) = tied(late, (early[1], early[-1]))
    late = across(jnp.sum(late.astype(F32), axis=0).astype(BF))
    arrived = [shift_by(mine, "h", 1), shift_by(other, "xl", 1), crossed(other)]
    late, (early, mine, other) = tied(late, (early, mine, other))
    late = jnp.broadcast_to(late[None], (plane, *late.shape))
    late = lax.all_to_all(late, PLANE, 0, 0, tiled=True).reshape(model, -1)

    grad_tokens = close(count, tokens, grad_mid, mine, *arrived, gains)
    early_far = [shift_by(e, "c", 1) for e in early]
    done = early_out(place, early, (), units, cols)
    grad_down, grad_up, grad_out = early_out(place, early_far, done, units, cols)
    done = late_out(place, late, (), units)
    grad_in, in_bias, up_bias, grad_gains, grad_shifts = late_out(
        place, shift_by(late, "c", 1), done, units
    )
    return (
        mixed,
        grad_tokens,
        grad_in,
        in_bias,
        grad_out,
        grad_up,
        up_bias.reshape(2, units),
        grad_down,
        grad_gains,
        grad_shifts,
    )


def solution(mesh):
    fine = Mesh(mesh.devices.reshape(4, 2, 4, 2, 2), ("z", "xl", "y", "c", "h"))
    blk = ("z", "xl", "y", "c")
    return jax.shard_map(
        local,
        mesh=fine,
        in_specs=(
            P(blk, None),
            P(None, blk, None),
            P(blk),
            P(None, None, "h"),
            P(None, "h"),
            P("h", None),
            P(None, "h"),
            P("h"),
            P("h", None),
            P(),
            P(),
        ),
        out_specs=(
            P(blk, None),
            P(None, blk, None),
            P(None, None, None, "h"),
            P(None, None, "h"),
            P(None, "h", None),
            P(None, None, "h"),
            P(None, "h"),
            P(None, "h", None),
            P(),
            P(),
        ),
        check_vma=False,
    )
```

profile of v0, /device:TPU:1, one launch (start us, length us, event | category | flops | bytes accessed | tf_op | source)
XLA Modules:
  0.0 310.9 jit_solution(7727464989599428512)
XLA Ops:
  0.7 2.4 front.1
  3.1 6.9 %all-to-all-start = ((bf16[8,208,512]{2,1,0:T(8,128)(2,1)}), bf16[8,208,512]{2,1,0:T(8,128)(2,1)S(1)}, u32[]{:S(2)}, u32[]{:S(2)}) async-start(bf16[8,208,512]{2,1,0:T(8,128)(2,1)} %get-tuple-element.125), calls=%async_computation | async-start | bytes 3407872 | tf_op jit(solution)/shard_map/all_to_all | solution.py:1122
  10.1 1.4 collective-permute-start.1
  11.4 2.6 collective-permute-start.2
  14.0 1.1 collective-permute-start.3
  15.1 1.8 collective-permute-start.4
  16.9 2.9 collective-permute-start
  20.8 2.3 collective-permute-done.2.refs_2_
  23.0 1.9 collective-permute-start.6
  24.9 4.2 %prepare.1 = (bf16[512,1536]{1,0:T(8,128)(2,1)}, f32[1,1536]{1,0:T(1,128)}, bf16[2,512,384]{2,1,0:T(8,128)(2,1)}, f32[512,128]{1,0:T(8,128)}, bf16[1040,512]{1,0:T(8,128)(2,1)}) custom-call(s32[1]{0:T(128)} %bitcast.1.place, bf16[3,512,256]{2,1,0:T(8,128)(2,1)} %in_weights.1, f32[2,256]{1,0:T(2,128)} %in_biases.1, f32[2,512]{1,0:T(2,128)} %gains.7, ...), custom_call_target="tpu_custom_call" | custom-call | flops 4000000000 | tf_op jit(solution)/shard_map/prepare/pallas_call | solution.py:78
  29.2 2.7 collective-permute-start.13
  33.2 1.2 copy-done.16
  34.4 22.8 %attend.1 = (bf16[192,384]{1,0:T(8,128)(2,1)}, bf16[192,384]{1,0:T(8,128)(2,1)}, bf16[192,384]{1,0:T(8,128)(2,1)}, bf16[192,384]{1,0:T(8,128)(2,1)}, bf16[4,192,...) custom-call(bf16[208,512]{1,0:T(8,128)(2,1)} %get-tuple-element.124., ...), custom_call_target="tpu_custom_call" | custom-call | flops 15000000512 | tf_op jit(solution)/shard_map/attend/pallas_call | solution.py:78
  58.3 1.7 collective-permute-done.8.refs_4_
  60.9 3.5 %pair_merge.1 = (bf16[192,384]{1,0:T(8,128)(2,1)}, bf16[192,384]{1,0:T(8,128)(2,1)}, bf16[192,384]{1,0:T(8,128)(2,1)}, bf16[192,384]{1,0:T(8,128)(2,1)}) custom-call(bf16[192,384]{1,0:T(8,128)(2,1)} %get-tuple-element.126.refs_0_, bf16[192,384]{1,0:T(8,128)(2,1)} %get-tuple-element.127.refs_1_, bf16[192,384]{1,0:T(8,128)(2,1)} %get-tuple-element.128.refs_2_, ...), custom_call_target="tpu_custom_call" | custom-call | flops 3000000000 | tf_op jit(solution)/shard_map/pair_merge/pallas_call | solution.py:78
  64.4 4.5 %collective-permute-start.10 = (bf16[192,384]{1,0:T(8,128)(2,1)}, bf16[192,384]{1,0:T(8,128)(2,1)S(1)}, u32[]{:S(2)}, u32[]{:S(2)}) collective-permute-start(bf16[192,384]{1,0:T(8,128)(2,1)} %get-tuple-element.133), channel_id=1, source_target_pairs={{0,8},{4,12},{8,0},{12,4},{1,9},{5,13},{9,1},{13,5},{2,10},{6,14},... | collective-permute-start | bytes 442376 | tf_op jit(solution)/shard_map/ppermute | solution.py:29
  68.8 2.7 collective-permute-start.9
  71.5 1.5 thumbs.1
  73.0 3.0 collective-permute-done.11.refs_3_
  76.0 1.5 merge.1
  77.5 2.7 collective-permute-start.12
  80.3 2.9 collective-permute-done.12.low_far
  83.2 7.3 %feed_forward.1 = (bf16[256,512]{1,0:T(8,128)(2,1)}, f32[2,256,512]{2,1,0:T(8,128)S(1)}, bf16[2,256,512]{2,1,0:T(8,128)(2,1)S(1)}, bf16[192,640]{1,0:T(8,128)(2,...) custom-call(bf16[256,512]{1,0:T(8,128)(2,1)S(1)} %copy-done, ...), custom_call_target="tpu_custom_call" | custom-call | flops 12000000000 | tf_op jit(solution)/shard_map/feed_forward/pallas_call | solution.py:78
  90.5 1.4 weight_grads.1
  91.9 2.3 collective-permute-start.22
  94.2 1.5 collective-permute-start.15
  95.7 1.8 collective-permute-start.16
  98.8 4.6 %thumbs_back.1.refs_14_.refs_8_ = bf16[2,2,256,384]{3,2,1,0:T(8,128)(2,1)S(1)} custom-call(s32[1]{0:T(128)} %get-tuple-element.118.counts, bf16[256,1536]{1,0:T(8,128)(2,1)S(1)} %get-tuple-element.153.x, bf16[2,256,512]{2,1,0:T(8,128)(2,1)S(1)} %get-tuple-element.154.mid_low, bf16[256,512]{1,0:T(8,128)(2,1)S(1)} %copy-done.4), custom_call_target="tpu_custom_call" | custom-call | flops 6000000000 | tf_op jit(solution)/shard_map/thumbs_back/pallas_call | solution.py:78
  103.8 5.1 %collective-permute-done.16.refs_2_ = bf16[192,640]{1,0:T(8,128)(2,1)S(1)} collective-permute-done((bf16[192,640]{1,0:T(8,128)(2,1)S(1)}, bf16[192,640]{1,0:T(8,128)(2,1)S(1)}, u32[]{:S(2)}, u32[]{:S(2)}) %collective-permute-start.16) | collective-permute-done | bytes 245792 | tf_op jit(solution)/shard_map/ppermute | solution.py:29
  110.2 2.0 add_convert_fusion
  113.2 5.0 %all-to-all-start.1 = ((bf16[16,32,2304]{2,1,0:T(8,128)(2,1)}), bf16[16,32,2304]{2,1,0:T(8,128)(2,1)S(1)}, u32[]{:S(2)}, u32[]{:S(2)}) async-start(bf16[16,32,2304]{2,1,0:T(8,128)(2,1)} %add_convert_fusion), calls=%async_computation.1 | async-start | bytes 4718592 | tf_op jit(solution)/shard_map/all_to_all | solution.py:1156
  118.3 47.0 %reverse.1 = (bf16[192,512]{1,0:T(8,128)(2,1)}, bf16[192,512]{1,0:T(8,128)(2,1)}, bf16[192,512]{1,0:T(8,128)(2,1)}, bf16[192,512]{1,0:T(8,128)(2,1)}, bf16[4,192...) custom-call(s32[16]{0:T(128)} %get-tuple-element.142.counts, ...), custom_call_target="tpu_custom_call" | custom-call | flops 44999999488 | tf_op jit(solution)/shard_map/reverse/pallas_call | solution.py:78
  165.9 2.7 collective-permute-start.26
  169.1 2.9 add_convert_fusion.1
  172.0 1.7 collective-permute-done.24
  174.5 3.5 %all-to-all-start.2 = ((bf16[4,32,2304]{2,1,0:T(8,128)(2,1)}), bf16[4,32,2304]{2,1,0:T(8,128)(2,1)S(1)}, u32[]{:S(2)}, u32[]{:S(2)}) async-start(bf16[4,32,2304]{2,1,0:T(8,128)(2,1)} %broadcast_in_dim.28), calls=%async_computation.2 | async-start | bytes 1179648 | tf_op jit(solution)/shard_map/all_to_all | solution.py:1166
  178.0 2.5 fold.1
  180.5 3.7 %collective-permute-start.28 = (bf16[192,512]{1,0:T(8,128)(2,1)}, bf16[192,512]{1,0:T(8,128)(2,1)S(1)}, u32[]{:S(2)}, u32[]{:S(2)}) collective-permute-start(bf16[192,512]{1,0:T(8,128)(2,1)} %get-tuple-element.186), channel_id=1, source_target_pairs={{0,12},{4,0},{8,4},{12,8},{1,13},{5,1},{9,5},{13,9},{2,14},{6,2},{... | collective-permute-start | bytes 589832 | tf_op jit(solution)/shard_map/ppermute | solution.py:29
  184.2 4.7 %collective-permute-start.29 = (bf16[192,512]{1,0:T(8,128)(2,1)}, bf16[192,512]{1,0:T(8,128)(2,1)S(1)}, u32[]{:S(2)}, u32[]{:S(2)}) collective-permute-start(bf16[192,512]{1,0:T(8,128)(2,1)} %get-tuple-element.187), channel_id=1, source_target_pairs={{0,8},{4,12},{8,0},{12,4},{1,9},{5,13},{9,1},{13,5},{2,10},{6,14},... | collective-permute-start | bytes 589832 | tf_op jit(solution)/shard_map/ppermute | solution.py:29
  189.8 2.7 collective-permute-done.29.refs_2_
  193.2 4.6 %collective-permute-done.30.refs_3_ = bf16[192,512]{1,0:T(8,128)(2,1)} collective-permute-done((bf16[192,512]{1,0:T(8,128)(2,1)}, bf16[192,512]{1,0:T(8,128)(2,1)}, u32[]{:S(2)}, u32[]{:S(2)}) %collective-permute-start.30) | collective-permute-done | bytes 196640 | tf_op jit(solution)/shard_map/ppermute | solution.py:29
  197.8 7.0 %all-to-all-start.3 = ((bf16[16,32,1024]{2,1,0:T(8,128)(2,1)}), bf16[16,32,1024]{2,1,0:T(8,128)(2,1)S(1)}, u32[]{:S(2)}, u32[]{:S(2)}) async-start(bf16[16,32,1024]{2,1,0:T(8,128)(2,1)} %bitcast.13), calls=%async_computation.3 | async-start | bytes 2097152 | tf_op jit(solution)/shard_map/all_to_all | solution.py:1174
  204.8 1.4 collective-permute-start.31
  206.1 1.4 collective-permute-start.32
  207.5 2.8 collective-permute-start.37
  210.3 1.5 collective-permute-start.36
  211.8 21.6 %collective-permute-done.31.refs_1_ = bf16[4,32,2304]{2,1,0:T(8,128)(2,1)S(1)} collective-permute-done((bf16[4,32,2304]{2,1,0:T(8,128)(2,1)S(1)}, bf16[4,32,2304]{2,1,0:T(8,128)(2,1)S(1)}, u32[]{:S(2)}, u32[]{:S(2)}) %collective-permute-start.31) | collective-permute-done | bytes 589856 | tf_op jit(solution)/shard_map/ppermute | solution.py:29
  234.5 1.3 collective-permute-start.34
  235.8 1.5 collective-permute-start.35
  237.3 5.3 %grad_one.1 = (bf16[2,256,512]{2,1,0:T(8,128)(2,1)}, bf16[2,192,512]{2,1,0:T(8,128)(2,1)}) custom-call(s32[1]{0:T(128)} %get-tuple-element.118.counts, bf16[192,512]{1,0:T(8,128)(2,1)} %get-tuple-element.194.refs_0_, bf16[192,512]{1,0:T(8,128)(2,1)} %copy-done.39, bf16[192,512]{1,0:T(8,128)(2,1)} %copy-done.40, ...), custom_call_target="tpu_custom_call" | custom-call | flops 5000000000 | tf_op jit(solution)/shard_map/grad_one/pallas_call | solution.py:78
  242.8 3.1 collective-permute-done.33
  245.9 1.1 broadcast_in_dim.32
  247.0 17.1 %all-to-all-start.4 = ((bf16[16,32,1024]{2,1,0:T(8,128)(2,1)}), bf16[16,32,1024]{2,1,0:T(8,128)(2,1)S(1)}, u32[]{:S(2)}, u32[]{:S(2)}) async-start(bf16[16,32,1024]{2,1,0:T(8,128)(2,1)} %broadcast_in_dim.32), calls=%async_computation.4 | async-start | bytes 2097152 | tf_op jit(solution)/shard_map/all_to_all | solution.py:1182
  265.0 2.7 collective-permute-start.38
  267.7 3.3 %collective-permute-start.42 = (bf16[4,32,2304]{2,1,0:T(8,128)(2,1)S(1)}, bf16[4,32,2304]{2,1,0:T(8,128)(2,1)S(1)}, u32[]{:S(2)}, u32[]{:S(2)}) collective-permute-start(bf16[4,32,2304]{2,1,0:T(8,128)(2,1)S(1)} %all-to-all-done.2.refs_0_), channel_id=1, source_target_pairs={{0,2},{2,0},{1,3},{3,1},{4,6},{6,4},{5,7},{7,5},{8,10},{10,8},{9,1... | collective-permute-start | bytes 1769480 | tf_op jit(solution)/shard_map/ppermute | solution.py:29
  271.1 1.5 collective-permute-done.39.side
  272.6 6.3 %collective-permute-start.44 = (bf16[4,32,2304]{2,1,0:T(8,128)(2,1)}, bf16[4,32,2304]{2,1,0:T(8,128)(2,1)}, u32[]{:S(2)}, u32[]{:S(2)}) collective-permute-start(bf16[4,32,2304]{2,1,0:T(8,128)(2,1)} %collective-permute-done.36.refs_2_), channel_id=1, source_target_pairs={{0,2},{2,0},{1,3},{3,1},{4,6},{6,4},{5,7},{7,5},{8,10},{10,8},{9,1... | collective-permute-start | bytes 1769480 | tf_op jit(solution)/shard_map/ppermute | solution.py:29
  279.7 9.6 %collective-permute-start.45 = (bf16[4,32,2304]{2,1,0:T(8,128)(2,1)}, bf16[4,32,2304]{2,1,0:T(8,128)(2,1)}, u32[]{:S(2)}, u32[]{:S(2)}) collective-permute-start(bf16[4,32,2304]{2,1,0:T(8,128)(2,1)} %collective-permute-done.32.refs_3_), channel_id=1, source_target_pairs={{0,2},{2,0},{1,3},{3,1},{4,6},{6,4},{5,7},{7,5},{8,10},{10,8},{9,1... | collective-permute-start | bytes 1769480 | tf_op jit(solution)/shard_map/ppermute | solution.py:29
  289.3 4.2 %early_own.1 = (f32[2,1024,512]{2,1,0:T(8,128)}, f32[2,512,1024]{2,1,0:T(8,128)}, f32[2,256,512]{2,1,0:T(8,128)}) custom-call(s32[11]{0:T(128)} %stack.44.place, bf16[4,32,2304]{2,1,0:T(8,128)(2,1)} %copy-done.18, bf16[4,32,2304]{2,1,0:T(8,128)(2,1)} %copy-done.22, bf16[4,32,2304]{2,1,0:T(8,128)(2,1)} %collective-permute-done.36.refs_2_, ...), custom_call_target="tpu_custom_call" | custom-call | flops 5000000000 | tf_op jit(solution)/shard_map/early_own/pallas_call | solution.py:989
  293.7 4.2 %close.1 = f32[2,256,512]{2,1,0:T(8,128)} custom-call(s32[1]{0:T(128)} %get-tuple-element.118.counts, bf16[256,512]{1,0:T(8,128)(2,1)} %tokens.7, f32[2,256,512]{2,1,0:T(8,128)} %copy-done.10, bf16[2,256,512]{2,1,0:T(8,128)(2,1)} %get-tuple-element.204.mine, bf16[2,256,512]{2,1,0:T(8,128)(2,1)} %collective-permute-done.38.head, ...), custom_call_target="tpu_custom_call" | custom-call | flops 4000000000 | tf_op jit(solution)/shard_map/close/pallas_call | solution.py:78
  298.7 4.2 %early_far.1 = (f32[2,1024,512]{2,1,0:T(8,128)}, f32[2,512,1024]{2,1,0:T(8,128)}, f32[2,256,512]{2,1,0:T(8,128)}) custom-call(s32[11]{0:T(128)} %stack.44.place, bf16[4,32,2304]{2,1,0:T(8,128)(2,1)} %copy-done.24, bf16[4,32,2304]{2,1,0:T(8,128)(2,1)} %collective-permute-done.43.refs_1_, ...), custom_call_target="tpu_custom_call", output_to_operand_aliasing={{0}: (5, {}), {1}: (6, {}), {2}: (7, {})} | custom-call | flops 5000000000 | tf_op jit(solution)/shard_map/early_far/pallas_call | solution.py:989
  302.9 2.6 late_own.1
  306.5 2.6 late_far.1
  309.1 1.3 copy.31
  (153 shorter events, 16.4 us)
Async XLA Ops:
  0.6 16.3 %copy-start.4 = (bf16[256,512]{1,0:T(8,128)(2,1)S(1)}, bf16[256,512]{1,0:T(8,128)(2,1)}, u32[]{:S(2)}) copy-start(bf16[256,512]{1,0:T(8,128)(2,1)} %out_weight.3) | copy-start | bytes 786436
  3.1 30.1 %all-to-all-start = ((bf16[8,208,512]{2,1,0:T(8,128)(2,1)}), bf16[8,208,512]{2,1,0:T(8,128)(2,1)S(1)}, u32[]{:S(2)}, u32[]{:S(2)}) async-start(bf16[8,208,512]{2,1,0:T(8,128)(2,1)} %get-tuple-element.125), calls=%async_computation | async-start | bytes 3407872 | tf_op jit(solution)/shard_map/all_to_all | solution.py:1122
  10.1 10.4 %collective-permute-start.1 = (bf16[208,512]{1,0:T(8,128)(2,1)S(1)}, bf16[208,512]{1,0:T(8,128)(2,1)}, u32[]{:S(2)}, u32[]{:S(2)}) collective-permute-start(bf16[208,512]{1,0:T(8,128)(2,1)S(1)} %copy-done.36), channel_id=1, source_target_pairs={{0,4},{4,8},{8,12},{12,0},{1,5},{5,9},{9,13},{13,1},{2,6},{6,10},{... | collective-permute-start | bytes 638984 | tf_op jit(solution)/shard_map/ppermute | solution.py:29
  11.4 11.6 %collective-permute-start.2 = (bf16[208,512]{1,0:T(8,128)(2,1)S(1)}, bf16[208,512]{1,0:T(8,128)(2,1)}, u32[]{:S(2)}, u32[]{:S(2)}) collective-permute-start(bf16[208,512]{1,0:T(8,128)(2,1)S(1)} %copy-done.36), channel_id=1, source_target_pairs={{0,8},{4,12},{8,0},{12,4},{1,9},{5,13},{9,1},{13,5},{2,10},{6,14},... | collective-permute-start | bytes 638984 | tf_op jit(solution)/shard_map/ppermute | solution.py:29
  14.0 10.9 %collective-permute-start.3 = (bf16[208,512]{1,0:T(8,128)(2,1)S(1)}, bf16[208,512]{1,0:T(8,128)(2,1)}, u32[]{:S(2)}, u32[]{:S(2)}) collective-permute-start(bf16[208,512]{1,0:T(8,128)(2,1)S(1)} %copy-done.36), channel_id=1, source_target_pairs={{0,12},{4,0},{8,4},{12,8},{1,13},{5,1},{9,5},{13,9},{2,14},{6,2},{... | collective-permute-start | bytes 638984 | tf_op jit(solution)/shard_map/ppermute | solution.py:29
  15.1 16.7 %collective-permute-start.4 = (bf16[208,512]{1,0:T(8,128)(2,1)S(1)}, bf16[208,512]{1,0:T(8,128)(2,1)}, u32[]{:S(2)}, u32[]{:S(2)}) collective-permute-start(bf16[208,512]{1,0:T(8,128)(2,1)S(1)} %copy-done.36), channel_id=1, source_target_pairs={{0,2},{2,0},{1,3},{3,1},{4,6},{6,4},{5,7},{7,5},{8,10},{10,8},{9,1... | collective-permute-start | bytes 638984 | tf_op jit(solution)/shard_map/ppermute | solution.py:29
  16.9 12.2 %collective-permute-start = (bf16[256,512]{1,0:T(8,128)(2,1)S(1)}, bf16[256,512]{1,0:T(8,128)(2,1)S(1)}, u32[]{:S(2)}, u32[]{:S(2)}) collective-permute-start(bf16[256,512]{1,0:T(8,128)(2,1)S(1)} %copy-done.4), channel_id=1, source_target_pairs={{0,17},{1,16},{16,1},{17,0},{2,19},{3,18},{18,3},{19,2},{4,21},{5,... | collective-permute-start | bytes 786440 | tf_op jit(solution)/shard_map/ppermute | solution.py:1083
  20.5 11.3 %collective-permute-start.5 = (bf16[208,512]{1,0:T(8,128)(2,1)}, bf16[208,512]{1,0:T(8,128)(2,1)S(1)}, u32[]{:S(2)}, u32[]{:S(2)}) collective-permute-start(bf16[208,512]{1,0:T(8,128)(2,1)} %collective-permute-done.1.refs_1_), channel_id=1, source_target_pairs={{0,2},{2,0},{1,3},{3,1},{4,6},{6,4},{5,7},{7,5},{8,10},{10,8},{9,1... | collective-permute-start | bytes 638984 | tf_op jit(solution)/shard_map/ppermute | solution.py:29
  23.0 8.8 %collective-permute-start.6 = (bf16[208,512]{1,0:T(8,128)(2,1)}, bf16[208,512]{1,0:T(8,128)(2,1)S(1)}, u32[]{:S(2)}, u32[]{:S(2)}) collective-permute-start(bf16[208,512]{1,0:T(8,128)(2,1)} %collective-permute-done.2.refs_2_), channel_id=1, source_target_pairs={{0,2},{2,0},{1,3},{3,1},{4,6},{6,4},{5,7},{7,5},{8,10},{10,8},{9,1... | collective-permute-start | bytes 638984 | tf_op jit(solution)/shard_map/ppermute | solution.py:29
  24.9 8.3 %collective-permute-start.7 = (bf16[208,512]{1,0:T(8,128)(2,1)}, bf16[208,512]{1,0:T(8,128)(2,1)}, u32[]{:S(2)}, u32[]{:S(2)}) collective-permute-start(bf16[208,512]{1,0:T(8,128)(2,1)} %collective-permute-done.3.refs_3_), channel_id=1, source_target_pairs={{0,2},{2,0},{1,3},{3,1},{4,6},{6,4},{5,7},{7,5},{8,10},{10,8},{9,1... | collective-permute-start | bytes 638984 | tf_op jit(solution)/shard_map/ppermute | solution.py:29
  29.2 29.0 %collective-permute-start.13 = (bf16[1040,512]{1,0:T(8,128)(2,1)}, bf16[1040,512]{1,0:T(8,128)(2,1)S(1)}, u32[]{:S(2)}, u32[]{:S(2)}) collective-permute-start(bf16[1040,512]{1,0:T(8,128)(2,1)} %get-tuple-element.139), channel_id=1, source_target_pairs={{0,17},{1,16},{16,1},{17,0},{2,19},{3,18},{18,3},{19,2},{4,21},{5,... | collective-permute-start | bytes 3194888 | tf_op jit(solution)/shard_map/ppermute | solution.py:1083
  57.2 2.8 collective-permute-start.8
  58.2 22.1 %collective-permute-start.14 = (bf16[1040,512]{1,0:T(8,128)(2,1)S(1)}, bf16[1040,512]{1,0:T(8,128)(2,1)S(1)}, u32[]{:S(2)}, u32[]{:S(2)}) collective-permute-start(bf16[1040,512]{1,0:T(8,128)(2,1)S(1)} %collective-permute-done.13.far_one), channel_id=1, source_target_pairs={{0,2},{2,0},{1,3},{3,1},{4,6},{6,4},{5,7},{7,5},{8,10},{10,8},{9,1... | collective-permute-start | bytes 3194888 | tf_op jit(solution)/shard_map/ppermute | solution.py:29
  60.8 10.7 %copy-start = (bf16[256,512]{1,0:T(8,128)(2,1)S(1)}, bf16[256,512]{1,0:T(8,128)(2,1)}, u32[]{:S(2)}) copy-start(bf16[256,512]{1,0:T(8,128)(2,1)} %tokens.7) | copy-start | bytes 786436
  60.8 10.7 %copy-start.6 = (f32[4,512]{1,0:T(4,128)S(1)}, f32[4,512]{1,0:T(4,128)}, u32[]{:S(2)}) copy-start(f32[4,512]{1,0:T(4,128)} %shifts.5) | copy-start | bytes 24580
  60.8 10.7 %copy-start.8 = (f32[2,512]{1,0:T(2,128)S(1)}, f32[2,512]{1,0:T(2,128)}, u32[]{:S(2)}) copy-start(f32[2,512]{1,0:T(2,128)} %gains.7) | copy-start | bytes 12292
  60.8 10.7 %copy-start.9 = (bf16[512,1536]{1,0:T(8,128)(2,1)S(1)}, bf16[512,1536]{1,0:T(8,128)(2,1)}, u32[]{:S(2)}) copy-start(bf16[512,1536]{1,0:T(8,128)(2,1)} %get-tuple-element.121.weights.refs_9_) | copy-start | bytes 4718596
  60.8 10.7 %copy-start.14 = (f32[1,1536]{1,0:T(1,128)S(1)}, f32[1,1536]{1,0:T(1,128)}, u32[]{:S(2)}) copy-start(f32[1,1536]{1,0:T(1,128)} %get-tuple-element.122.biases.refs_10_) | copy-start | bytes 18436
  64.4 8.6 %collective-permute-start.10 = (bf16[192,384]{1,0:T(8,128)(2,1)}, bf16[192,384]{1,0:T(8,128)(2,1)S(1)}, u32[]{:S(2)}, u32[]{:S(2)}) collective-permute-start(bf16[192,384]{1,0:T(8,128)(2,1)} %get-tuple-element.133), channel_id=1, source_target_pairs={{0,8},{4,12},{8,0},{12,4},{1,9},{5,13},{9,1},{13,5},{2,10},{6,14},... | collective-permute-start | bytes 442376 | tf_op jit(solution)/shard_map/ppermute | solution.py:29
  68.8 7.1 %collective-permute-start.11 = (bf16[192,384]{1,0:T(8,128)(2,1)}, bf16[192,384]{1,0:T(8,128)(2,1)S(1)}, u32[]{:S(2)}, u32[]{:S(2)}) collective-permute-start(bf16[192,384]{1,0:T(8,128)(2,1)} %get-tuple-element.134), channel_id=1, source_target_pairs={{0,4},{4,8},{8,12},{12,0},{1,5},{5,9},{9,13},{13,1},{2,6},{6,10},{... | collective-permute-start | bytes 442376 | tf_op jit(solution)/shard_map/ppermute | solution.py:29
  68.8 7.1 %collective-permute-start.9 = (bf16[192,384]{1,0:T(8,128)(2,1)}, bf16[192,384]{1,0:T(8,128)(2,1)S(1)}, u32[]{:S(2)}, u32[]{:S(2)}) collective-permute-start(bf16[192,384]{1,0:T(8,128)(2,1)} %get-tuple-element.132), channel_id=1, source_target_pairs={{0,12},{4,0},{8,4},{12,8},{1,13},{5,1},{9,5},{13,9},{2,14},{6,2},{... | collective-permute-start | bytes 442376 | tf_op jit(solution)/shard_map/ppermute | solution.py:29
  77.5 5.6 %collective-permute-start.12 = (bf16[256,256]{1,0:T(8,128)(2,1)S(1)}, bf16[256,256]{1,0:T(8,128)(2,1)S(1)}, u32[]{:S(2)}, u32[]{:S(2)}) collective-permute-start(bf16[256,256]{1,0:T(8,128)(2,1)S(1)} %get-tuple-element.135.low), channel_id=1, source_target_pairs={{0,1},{1,0},{2,3},{3,2},{4,5},{5,4},{6,7},{7,6},{8,9},{9,8},{10,11... | collective-permute-start | bytes 393224 | tf_op jit(solution)/shard_map/ppermute | solution.py:29
  91.9 18.3 %collective-permute-start.22 = (bf16[16,32,2304]{2,1,0:T(8,128)(2,1)S(1)}, bf16[16,32,2304]{2,1,0:T(8,128)(2,1)S(1)}, u32[]{:S(2)}, u32[]{:S(2)}) collective-permute-start(bf16[16,32,2304]{2,1,0:T(8,128)(2,1)S(1)} %get-tuple-element.152), channel_id=1, source_target_pairs={{0,2},{2,0},{1,3},{3,1},{4,6},{6,4},{5,7},{7,5},{8,10},{10,8},{9,1... | collective-permute-start | bytes 7077896 | tf_op jit(solution)/shard_map/ppermute | solution.py:29
  94.2 9.3 %collective-permute-start.15 = (bf16[192,640]{1,0:T(8,128)(2,1)S(1)}, bf16[192,640]{1,0:T(8,128)(2,1)S(1)}, u32[]{:S(2)}, u32[]{:S(2)}) collective-permute-start(bf16[192,640]{1,0:T(8,128)(2,1)S(1)} %get-tuple-element.155.refs_0_), channel_id=1, source_target_pairs={{0,4},{4,8},{8,12},{12,0},{1,5},{5,9},{9,13},{13,1},{2,6},{6,10},{... | collective-permute-start | bytes 737288 | tf_op jit(solution)/shard_map/ppermute | solution.py:29
  95.7 13.2 %collective-permute-start.16 = (bf16[192,640]{1,0:T(8,128)(2,1)S(1)}, bf16[192,640]{1,0:T(8,128)(2,1)S(1)}, u32[]{:S(2)}, u32[]{:S(2)}) collective-permute-start(bf16[192,640]{1,0:T(8,128)(2,1)S(1)} %get-tuple-element.155.refs_0_), channel_id=1, source_target_pairs={{0,8},{4,12},{8,0},{12,4},{1,9},{5,13},{9,1},{13,5},{2,10},{6,14},... | collective-permute-start | bytes 737288 | tf_op jit(solution)/shard_map/ppermute | solution.py:29
  97.6 12.2 %collective-permute-start.17 = (bf16[192,640]{1,0:T(8,128)(2,1)S(1)}, bf16[192,640]{1,0:T(8,128)(2,1)S(1)}, u32[]{:S(2)}, u32[]{:S(2)}) collective-permute-start(bf16[192,640]{1,0:T(8,128)(2,1)S(1)} %get-tuple-element.155.refs_0_), channel_id=1, source_target_pairs={{0,12},{4,0},{8,4},{12,8},{1,13},{5,1},{9,5},{13,9},{2,14},{6,2},{... | collective-permute-start | bytes 737288 | tf_op jit(solution)/shard_map/ppermute | solution.py:29
  98.1 14.2 %collective-permute-start.18 = (bf16[192,640]{1,0:T(8,128)(2,1)S(1)}, bf16[192,640]{1,0:T(8,128)(2,1)S(1)}, u32[]{:S(2)}, u32[]{:S(2)}) collective-permute-start(bf16[192,640]{1,0:T(8,128)(2,1)S(1)} %get-tuple-element.155.refs_0_), channel_id=1, source_target_pairs={{0,2},{2,0},{1,3},{3,1},{4,6},{6,4},{5,7},{7,5},{8,10},{10,8},{9,1... | collective-permute-start | bytes 737288 | tf_op jit(solution)/shard_map/ppermute | solution.py:29
  103.4 8.8 %copy-start.11 = (bf16[2,2,256,384]{3,2,1,0:T(8,128)(2,1)}, bf16[2,2,256,384]{3,2,1,0:T(8,128)(2,1)S(1)}, u32[]{:S(2)}) copy-start(bf16[2,2,256,384]{3,2,1,0:T(8,128)(2,1)S(1)} %thumbs_back.1.refs_14_.refs_8_) | copy-start | bytes 2359300
  103.5 8.8 %collective-permute-start.19 = (bf16[192,640]{1,0:T(8,128)(2,1)S(1)}, bf16[192,640]{1,0:T(8,128)(2,1)S(1)}, u32[]{:S(2)}, u32[]{:S(2)}) collective-permute-start(bf16[192,640]{1,0:T(8,128)(2,1)S(1)} %collective-permute-done.15.refs_1_), channel_id=1, source_target_pairs={{0,2},{2,0},{1,3},{3,1},{4,6},{6,4},{5,7},{7,5},{8,10},{10,8},{9,1... | collective-permute-start | bytes 737288 | tf_op jit(solution)/shard_map/ppermute | solution.py:29
  108.9 3.4 %collective-permute-start.20 = (bf16[192,640]{1,0:T(8,128)(2,1)S(1)}, bf16[192,640]{1,0:T(8,128)(2,1)S(1)}, u32[]{:S(2)}, u32[]{:S(2)}) collective-permute-start(bf16[192,640]{1,0:T(8,128)(2,1)S(1)} %collective-permute-done.16.refs_2_), channel_id=1, source_target_pairs={{0,2},{2,0},{1,3},{3,1},{4,6},{6,4},{5,7},{7,5},{8,10},{10,8},{9,1... | collective-permute-start | bytes 737288 | tf_op jit(solution)/shard_map/ppermute | solution.py:29
  109.7 2.6 collective-permute-start.21
  113.2 55.4 %all-to-all-start.1 = ((bf16[16,32,2304]{2,1,0:T(8,128)(2,1)}), bf16[16,32,2304]{2,1,0:T(8,128)(2,1)S(1)}, u32[]{:S(2)}, u32[]{:S(2)}) async-start(bf16[16,32,2304]{2,1,0:T(8,128)(2,1)} %add_convert_fusion), calls=%async_computation.1 | async-start | bytes 4718592 | tf_op jit(solution)/shard_map/all_to_all | solution.py:1156
  165.3 3.7 %collective-permute-start.23 = (bf16[512,1024]{1,0:T(8,128)(2,1)}, bf16[512,1024]{1,0:T(8,128)(2,1)}, u32[]{:S(2)}, u32[]{:S(2)}) collective-permute-start(bf16[512,1024]{1,0:T(8,128)(2,1)} %get-tuple-element.174), channel_id=1, source_target_pairs={{0,2},{2,0},{1,3},{3,1},{4,6},{6,4},{5,7},{7,5},{8,10},{10,8},{9,1... | collective-permute-start | bytes 3145736 | tf_op jit(solution)/shard_map/ppermute | solution.py:29
  165.7 12.3 %collective-permute-start.27 = (bf16[4,192,512]{2,1,0:T(8,128)(2,1)}, bf16[4,192,512]{2,1,0:T(8,128)(2,1)}, u32[]{:S(2)}, u32[]{:S(2)}) collective-permute-start(bf16[4,192,512]{2,1,0:T(8,128)(2,1)} %get-tuple-element.184), channel_id=1, source_target_pairs={{0,2},{2,0},{1,3},{3,1},{4,6},{6,4},{5,7},{7,5},{8,10},{10,8},{9,1... | collective-permute-start | bytes 2359304 | tf_op jit(solution)/shard_map/ppermute | solution.py:29
  165.9 23.8 %collective-permute-start.25 = (bf16[2,192,1024]{2,1,0:T(8,128)(2,1)}, bf16[2,192,1024]{2,1,0:T(8,128)(2,1)S(1)}, u32[]{:S(2)}, u32[]{:S(2)}) collective-permute-start(bf16[2,192,1024]{2,1,0:T(8,128)(2,1)} %get-tuple-element.178), channel_id=1, source_target_pairs={{0,32},{32,64},{64,96},{96,0},{1,33},{33,65},{65,97},{97,1},{2,34}... | collective-permute-start | bytes 2359304 | tf_op jit(solution)/shard_map/ppermute | solution.py:29
  165.9 23.8 %collective-permute-start.26 = (bf16[2,192,1024]{2,1,0:T(8,128)(2,1)}, bf16[2,192,1024]{2,1,0:T(8,128)(2,1)}, u32[]{:S(2)}, u32[]{:S(2)}) collective-permute-start(bf16[2,192,1024]{2,1,0:T(8,128)(2,1)} %get-tuple-element.179), channel_id=1, source_target_pairs={{0,96},{32,0},{64,32},{96,64},{1,97},{33,1},{65,33},{97,65},{2,98}... | collective-permute-start | bytes 2359304 | tf_op jit(solution)/shard_map/ppermute | solution.py:29
  169.0 4.7 %collective-permute-start.24 = (bf16[32,2304]{1,0:T(8,128)(2,1)S(1)}, bf16[32,2304]{1,0:T(8,128)(2,1)S(1)}, u32[]{:S(2)}, u32[]{:S(2)}) collective-permute-start(bf16[32,2304]{1,0:T(8,128)(2,1)S(1)} %reduce_sum.24), channel_id=1, source_target_pairs={{0,16},{16,0},{1,17},{17,1},{2,18},{18,2},{3,19},{19,3},{4,20},{20... | collective-permute-start | bytes 442376 | tf_op jit(solution)/shard_map/ppermute | solution.py:29
  174.5 23.3 %all-to-all-start.2 = ((bf16[4,32,2304]{2,1,0:T(8,128)(2,1)}), bf16[4,32,2304]{2,1,0:T(8,128)(2,1)S(1)}, u32[]{:S(2)}, u32[]{:S(2)}) async-start(bf16[4,32,2304]{2,1,0:T(8,128)(2,1)} %broadcast_in_dim.28), calls=%async_computation.2 | async-start | bytes 1179648 | tf_op jit(solution)/shard_map/all_to_all | solution.py:1166
  178.0 29.5 %copy-start.20 = (bf16[2,192,1024]{2,1,0:T(8,128)(2,1)S(1)}, bf16[2,192,1024]{2,1,0:T(8,128)(2,1)}, u32[]{:S(2)}) copy-start(bf16[2,192,1024]{2,1,0:T(8,128)(2,1)} %get-tuple-element.200) | copy-start | bytes 2359300
  180.5 9.2 %collective-permute-start.28 = (bf16[192,512]{1,0:T(8,128)(2,1)}, bf16[192,512]{1,0:T(8,128)(2,1)S(1)}, u32[]{:S(2)}, u32[]{:S(2)}) collective-permute-start(bf16[192,512]{1,0:T(8,128)(2,1)} %get-tuple-element.186), channel_id=1, source_target_pairs={{0,12},{4,0},{8,4},{12,8},{1,13},{5,1},{9,5},{13,9},{2,14},{6,2},{... | collective-permute-start | bytes 589832 | tf_op jit(solution)/shard_map/ppermute | solution.py:29
  184.2 8.3 %collective-permute-start.29 = (bf16[192,512]{1,0:T(8,128)(2,1)}, bf16[192,512]{1,0:T(8,128)(2,1)S(1)}, u32[]{:S(2)}, u32[]{:S(2)}) collective-permute-start(bf16[192,512]{1,0:T(8,128)(2,1)} %get-tuple-element.187), channel_id=1, source_target_pairs={{0,8},{4,12},{8,0},{12,4},{1,9},{5,13},{9,1},{13,5},{2,10},{6,14},... | collective-permute-start | bytes 589832 | tf_op jit(solution)/shard_map/ppermute | solution.py:29
  188.9 8.9 %collective-permute-start.30 = (bf16[192,512]{1,0:T(8,128)(2,1)}, bf16[192,512]{1,0:T(8,128)(2,1)}, u32[]{:S(2)}, u32[]{:S(2)}) collective-permute-start(bf16[192,512]{1,0:T(8,128)(2,1)} %get-tuple-element.188), channel_id=1, source_target_pairs={{0,4},{4,8},{8,12},{12,0},{1,5},{5,9},{9,13},{13,1},{2,6},{6,10},{... | collective-permute-start | bytes 589832 | tf_op jit(solution)/shard_map/ppermute | solution.py:29
  189.7 47.6 %copy-start.21 = (bf16[2,192,1024]{2,1,0:T(8,128)(2,1)}, bf16[2,192,1024]{2,1,0:T(8,128)(2,1)S(1)}, u32[]{:S(2)}) copy-start(bf16[2,192,1024]{2,1,0:T(8,128)(2,1)S(1)} %collective-permute-done.25.refs_5_) | copy-start | bytes 2359300
  189.8 17.8 %copy-start.39 = (bf16[192,512]{1,0:T(8,128)(2,1)}, bf16[192,512]{1,0:T(8,128)(2,1)S(1)}, u32[]{:S(2)}) copy-start(bf16[192,512]{1,0:T(8,128)(2,1)S(1)} %collective-permute-done.28.refs_1_) | copy-start | bytes 589828
  197.8 69.9 %copy-start.18 = (bf16[4,32,2304]{2,1,0:T(8,128)(2,1)}, bf16[4,32,2304]{2,1,0:T(8,128)(2,1)S(1)}, u32[]{:S(2)}) copy-start(bf16[4,32,2304]{2,1,0:T(8,128)(2,1)S(1)} %all-to-all-done.2.refs_0_) | copy-start | bytes 1769476
  197.8 36.5 %all-to-all-start.3 = ((bf16[16,32,1024]{2,1,0:T(8,128)(2,1)}), bf16[16,32,1024]{2,1,0:T(8,128)(2,1)S(1)}, u32[]{:S(2)}, u32[]{:S(2)}) async-start(bf16[16,32,1024]{2,1,0:T(8,128)(2,1)} %bitcast.13), calls=%async_computation.3 | async-start | bytes 2097152 | tf_op jit(solution)/shard_map/all_to_all | solution.py:1174
  204.8 28.7 %collective-permute-start.31 = (bf16[4,32,2304]{2,1,0:T(8,128)(2,1)S(1)}, bf16[4,32,2304]{2,1,0:T(8,128)(2,1)S(1)}, u32[]{:S(2)}, u32[]{:S(2)}) collective-permute-start(bf16[4,32,2304]{2,1,0:T(8,128)(2,1)S(1)} %all-to-all-done.2.refs_0_), channel_id=1, source_target_pairs={{0,4},{4,8},{8,12},{12,0},{1,5},{5,9},{9,13},{13,1},{2,6},{6,10},{... | collective-permute-start | bytes 1769480 | tf_op jit(solution)/shard_map/ppermute | solution.py:29
  206.1 28.1 %collective-permute-start.32 = (bf16[4,32,2304]{2,1,0:T(8,128)(2,1)S(1)}, bf16[4,32,2304]{2,1,0:T(8,128)(2,1)}, u32[]{:S(2)}, u32[]{:S(2)}) collective-permute-start(bf16[4,32,2304]{2,1,0:T(8,128)(2,1)S(1)} %all-to-all-done.2.refs_0_), channel_id=1, source_target_pairs={{0,12},{4,0},{8,4},{12,8},{1,13},{5,1},{9,5},{13,9},{2,14},{6,2},{... | collective-permute-start | bytes 1769480 | tf_op jit(solution)/shard_map/ppermute | solution.py:29
  207.5 29.8 %collective-permute-start.37 = (bf16[2,192,1024]{2,1,0:T(8,128)(2,1)S(1)}, bf16[2,192,1024]{2,1,0:T(8,128)(2,1)}, u32[]{:S(2)}, u32[]{:S(2)}) collective-permute-start(bf16[2,192,1024]{2,1,0:T(8,128)(2,1)S(1)} %copy-done.20), channel_id=1, source_target_pairs={{0,64},{32,96},{64,0},{96,32},{1,65},{33,97},{65,1},{97,33},{2,66}... | collective-permute-start | bytes 2359304 | tf_op jit(solution)/shard_map/ppermute | solution.py:29
  210.3 35.5 %collective-permute-start.36 = (bf16[4,32,2304]{2,1,0:T(8,128)(2,1)S(1)}, bf16[4,32,2304]{2,1,0:T(8,128)(2,1)}, u32[]{:S(2)}, u32[]{:S(2)}) collective-permute-start(bf16[4,32,2304]{2,1,0:T(8,128)(2,1)S(1)} %all-to-all-done.2.refs_0_), channel_id=1, source_target_pairs={{0,8},{4,12},{8,0},{12,4},{1,9},{5,13},{9,1},{13,5},{2,10},{6,14},... | collective-permute-start | bytes 1769480 | tf_op jit(solution)/shard_map/ppermute | solution.py:29
  234.5 8.2 %collective-permute-start.34 = (bf16[32,256]{1,0:T(8,128)(2,1)S(1)}, bf16[32,256]{1,0:T(8,128)(2,1)S(1)}, u32[]{:S(2)}, u32[]{:S(2)}) collective-permute-start(bf16[32,256]{1,0:T(8,128)(2,1)S(1)} %pad_maximum_fusion), channel_id=1, source_target_pairs={{0,1},{1,0},{2,3},{3,2},{4,5},{5,4},{6,7},{7,6},{8,9},{9,8},{10,11... | collective-permute-start | bytes 49160 | tf_op jit(solution)/shard_map/ppermute | solution.py:29
  235.8 6.9 %collective-permute-start.35 = (bf16[32,256]{1,0:T(8,128)(2,1)S(1)}, bf16[32,256]{1,0:T(8,128)(2,1)S(1)}, u32[]{:S(2)}, u32[]{:S(2)}) collective-permute-start(bf16[32,256]{1,0:T(8,128)(2,1)S(1)} %pad_maximum_fusion), channel_id=1, source_target_pairs={{0,17},{1,16},{16,1},{17,0},{2,19},{3,18},{18,3},{19,2},{4,21},{5,... | collective-permute-start | bytes 49160 | tf_op jit(solution)/shard_map/ppermute | solution.py:1083
  242.6 21.5 %copy-start.26 = (bf16[2,192,512]{2,1,0:T(8,128)(2,1)S(1)}, bf16[2,192,512]{2,1,0:T(8,128)(2,1)}, u32[]{:S(2)}) copy-start(bf16[2,192,512]{2,1,0:T(8,128)(2,1)} %get-tuple-element.203) | copy-start | bytes 1179652
  242.6 28.4 %copy-start.23 = (bf16[4,32,2304]{2,1,0:T(8,128)(2,1)S(1)}, bf16[4,32,2304]{2,1,0:T(8,128)(2,1)}, u32[]{:S(2)}) copy-start(bf16[4,32,2304]{2,1,0:T(8,128)(2,1)} %copy-done.22) | copy-start | bytes 1769476
  242.6 3.2 %collective-permute-start.33 = (bf16[32,1024]{1,0:T(8,128)(2,1)S(1)}, bf16[32,1024]{1,0:T(8,128)(2,1)S(1)}, u32[]{:S(2)}, u32[]{:S(2)}) collective-permute-start(bf16[32,1024]{1,0:T(8,128)(2,1)S(1)} %reduce_sum.25), channel_id=1, source_target_pairs={{0,16},{16,0},{1,17},{17,1},{2,18},{18,2},{3,19},{19,3},{4,20},{20... | collective-permute-start | bytes 196616 | tf_op jit(solution)/shard_map/ppermute | solution.py:29
  247.0 46.6 %all-to-all-start.4 = ((bf16[16,32,1024]{2,1,0:T(8,128)(2,1)}), bf16[16,32,1024]{2,1,0:T(8,128)(2,1)S(1)}, u32[]{:S(2)}, u32[]{:S(2)}) async-start(bf16[16,32,1024]{2,1,0:T(8,128)(2,1)} %broadcast_in_dim.32), calls=%async_computation.4 | async-start | bytes 2097152 | tf_op jit(solution)/shard_map/all_to_all | solution.py:1182
  264.1 8.5 %collective-permute-start.39 = (bf16[2,192,512]{2,1,0:T(8,128)(2,1)S(1)}, bf16[2,192,512]{2,1,0:T(8,128)(2,1)S(1)}, u32[]{:S(2)}, u32[]{:S(2)}) collective-permute-start(bf16[2,192,512]{2,1,0:T(8,128)(2,1)S(1)} %copy-done.26), channel_id=1, source_target_pairs={{0,16},{16,0},{1,17},{17,1},{2,18},{18,2},{3,19},{19,3},{4,20},{20... | collective-permute-start | bytes 1179656 | tf_op jit(solution)/shard_map/ppermute | solution.py:29
  264.5 14.5 %collective-permute-start.40 = (bf16[2,192,512]{2,1,0:T(8,128)(2,1)S(1)}, bf16[2,192,512]{2,1,0:T(8,128)(2,1)S(1)}, u32[]{:S(2)}, u32[]{:S(2)}) collective-permute-start(bf16[2,192,512]{2,1,0:T(8,128)(2,1)S(1)} %copy-done.26), channel_id=1, source_target_pairs={{0,17},{1,16},{16,1},{17,0},{2,19},{3,18},{18,3},{19,2},{4,21},{5,... | collective-permute-start | bytes 1179656 | tf_op jit(solution)/shard_map/ppermute | solution.py:1083
  265.0 28.5 %collective-permute-start.38 = (bf16[2,256,512]{2,1,0:T(8,128)(2,1)}, bf16[2,256,512]{2,1,0:T(8,128)(2,1)}, u32[]{:S(2)}, u32[]{:S(2)}) collective-permute-start(bf16[2,256,512]{2,1,0:T(8,128)(2,1)} %get-tuple-element.204.mine), channel_id=1, source_target_pairs={{0,1},{1,0},{2,3},{3,2},{4,5},{5,4},{6,7},{7,6},{8,9},{9,8},{10,11... | collective-permute-start | bytes 1572872 | tf_op jit(solution)/shard_map/ppermute | solution.py:29
  267.7 30.1 %collective-permute-start.42 = (bf16[4,32,2304]{2,1,0:T(8,128)(2,1)S(1)}, bf16[4,32,2304]{2,1,0:T(8,128)(2,1)S(1)}, u32[]{:S(2)}, u32[]{:S(2)}) collective-permute-start(bf16[4,32,2304]{2,1,0:T(8,128)(2,1)S(1)} %all-to-all-done.2.refs_0_), channel_id=1, source_target_pairs={{0,2},{2,0},{1,3},{3,1},{4,6},{6,4},{5,7},{7,5},{8,10},{10,8},{9,1... | collective-permute-start | bytes 1769480 | tf_op jit(solution)/shard_map/ppermute | solution.py:29
  271.0 26.9 %collective-permute-start.43 = (bf16[4,32,2304]{2,1,0:T(8,128)(2,1)S(1)}, bf16[4,32,2304]{2,1,0:T(8,128)(2,1)}, u32[]{:S(2)}, u32[]{:S(2)}) collective-permute-start(bf16[4,32,2304]{2,1,0:T(8,128)(2,1)S(1)} %copy-done.23), channel_id=1, source_target_pairs={{0,2},{2,0},{1,3},{3,1},{4,6},{6,4},{5,7},{7,5},{8,10},{10,8},{9,1... | collective-permute-start | bytes 1769480 | tf_op jit(solution)/shard_map/ppermute | solution.py:29
  272.6 25.3 %collective-permute-start.44 = (bf16[4,32,2304]{2,1,0:T(8,128)(2,1)}, bf16[4,32,2304]{2,1,0:T(8,128)(2,1)}, u32[]{:S(2)}, u32[]{:S(2)}) collective-permute-start(bf16[4,32,2304]{2,1,0:T(8,128)(2,1)} %collective-permute-done.36.refs_2_), channel_id=1, source_target_pairs={{0,2},{2,0},{1,3},{3,1},{4,6},{6,4},{5,7},{7,5},{8,10},{10,8},{9,1... | collective-permute-start | bytes 1769480 | tf_op jit(solution)/shard_map/ppermute | solution.py:29
  279.7 18.2 %collective-permute-start.45 = (bf16[4,32,2304]{2,1,0:T(8,128)(2,1)}, bf16[4,32,2304]{2,1,0:T(8,128)(2,1)}, u32[]{:S(2)}, u32[]{:S(2)}) collective-permute-start(bf16[4,32,2304]{2,1,0:T(8,128)(2,1)} %collective-permute-done.32.refs_3_), channel_id=1, source_target_pairs={{0,2},{2,0},{1,3},{3,1},{4,6},{6,4},{5,7},{7,5},{8,10},{10,8},{9,1... | collective-permute-start | bytes 1769480 | tf_op jit(solution)/shard_map/ppermute | solution.py:29
  293.6 12.0 %collective-permute-start.41 = (bf16[512,1024]{1,0:T(8,128)(2,1)S(1)}, bf16[512,1024]{1,0:T(8,128)(2,1)S(1)}, u32[]{:S(2)}, u32[]{:S(2)}) collective-permute-start(bf16[512,1024]{1,0:T(8,128)(2,1)S(1)} %bitcast.20), channel_id=1, source_target_pairs={{0,2},{2,0},{1,3},{3,1},{4,6},{6,4},{5,7},{7,5},{8,10},{10,8},{9,1... | collective-permute-start | bytes 3145736 | tf_op jit(solution)/shard_map/ppermute | solution.py:29
  (28 other events, 93.9 us)
where the time goes:
time: 314 us; the launch traced here: 311 us
  Pallas kernels  122 us (39%)
  starting transfers between devices  119 us (38%)
  waiting for transfers between devices  50.2 us (16%)
  local copies, waits for them, and re-layouts  12.3 us (4%)
  other arithmetic  5.56 us (2%)
    pallas_call x13, Pallas kernels, local_call(): pl.pallas_call(body, out_shape=out, in_specs=ins, out_specs=outs, scratch...  108 us
    ppermute x42, starting transfers between devices, shift_by(): lax.ppermute(array, axis, [(i, (i + step) % size) for i in range(size)])  71.9 us
    ppermute x42, waiting for transfers between devices, shift_by(): lax.ppermute(array, axis, [(i, (i + step) % size) for i in range(size)])  50.2 us
    all_to_all x1, starting transfers between devices, local(): late = lax.all_to_all(late, PLANE, 0, 0, tiled=True).reshape(model, -1)  17.1 us
    unnamed x83, local copies, waits for them, and re-layouts  9.66 us
    pallas_call x2, Pallas kernels, early_out(): pl.pallas_call(functools.partial(early_kernel, len(parts), bool(before)),...  8.47 us
    ppermute x4, starting transfers between devices, crossed(): return lax.ppermute(array, ('xl', 'h'), [(i, n - 1 - i) for i in range(n)])  7.62 us
    all_to_all x1, starting transfers between devices, local(): late = lax.all_to_all(late, PLANE, 0, 0, tiled=True)  6.97 us
  transfers between devices with their start and end apart: 51, of which 11 were waited for; matrix products, arithmetic and copies ran while one was open for 2% of the time, Pallas kernels for 35%

commit v1 on v0

--- a/solution.py
+++ b/solution.py
@@ -1177,7 +1177,6 @@
     late, (early[1], early[-1]) = tied(late, (early[1], early[-1]))
     late = across(jnp.sum(late.astype(F32), axis=0).astype(BF))
     arrived = [shift_by(mine, "h", 1), shift_by(other, "xl", 1), crossed(other)]
-    late, (early, mine, other) = tied(late, (early, mine, other))
     late = jnp.broadcast_to(late[None], (plane, *late.shape))
     late = lax.all_to_all(late, PLANE, 0, 0, tiled=True).reshape(model, -1)
 

time: 314 us -> 308 us (0.981)
  waiting for transfers between devices: 50.2 us -> 70.3 us
  starting transfers between devices: 119 us -> 99.9 us
  Pallas kernels: 122 us -> 113 us
    ppermute x4, waiting for transfers between devices: 0.01 us -> 15.5 us  [crossed(): return lax.ppermute(array, ('xl', 'h'), [(i, n - 1 - i) for i in range(n)])]
    all_to_all x1, starting transfers between devices: 17.1 us -> 5.01 us  [local(): late = lax.all_to_all(late, PLANE, 0, 0, tiled=True).reshape(model, -1)]
    pallas_call x13, Pallas kernels: 108 us -> 99 us  [local_call(): pl.pallas_call(body, out_shape=out, in_specs=ins, out_specs=outs, scratch...]
    ppermute x42, starting transfers between devices: 71.9 us -> 63.9 us  [shift_by(): lax.ppermute(array, axis, [(i, (i + step) % size) for i in range(size)])]
    ppermute x42, waiting for transfers between devices: 50.2 us -> 54.8 us  [shift_by(): lax.ppermute(array, axis, [(i, (i + step) % size) for i in range(size)])]
  transfers between devices with their start and end apart: 51 -> 51, of which waited for: 11 -> 18; matrix products, arithmetic and copies ran while one was open for 2% -> 3% of each run, Pallas kernels for 35% -> 33%
where the time goes in v1:
time: 308 us; the launch traced here: 302 us
  Pallas kernels  113 us (37%)
  starting transfers between devices  99.9 us (32%)
  waiting for transfers between devices  70.3 us (23%)
  local copies, waits for them, and re-layouts  12.3 us (4%)
  other arithmetic  5.56 us (2%)
    pallas_call x13, Pallas kernels, local_call(): pl.pallas_call(body, out_shape=out, in_specs=ins, out_specs=outs, scratch...  99 us
    ppermute x42, starting transfers between devices, shift_by(): lax.ppermute(array, axis, [(i, (i + step) % size) for i in range(size)])  63.9 us
    ppermute x42, waiting for transfers between devices, shift_by(): lax.ppermute(array, axis, [(i, (i + step) % size) for i in range(size)])  54.8 us
    ppermute x4, waiting for transfers between devices, crossed(): return lax.ppermute(array, ('xl', 'h'), [(i, n - 1 - i) for i in range(n)])  15.5 us
    unnamed x83, local copies, waits for them, and re-layouts  9.69 us
    ppermute x4, starting transfers between devices, crossed(): return lax.ppermute(array, ('xl', 'h'), [(i, n - 1 - i) for i in range(n)])  8.53 us
    pallas_call x2, Pallas kernels, early_out(): pl.pallas_call(functools.partial(early_kernel, len(parts), bool(before)),...  8.47 us
    all_to_all x1, starting transfers between devices, local(): early = lax.all_to_all(early, PLANE, 0, 0, tiled=True)  7.58 us
  transfers between devices with their start and end apart: 51, of which 18 were waited for; matrix products, arithmetic and copies ran while one was open for 3% of the time, Pallas kernels for 33%

profile of v1, /device:TPU:1, one launch (start us, length us, event | category | flops | bytes accessed | tf_op | source)
XLA Modules:
  0.0 302.4 jit_solution(15208737318665621198)
XLA Ops:
  0.7 2.4 front.1
  3.1 6.9 %all-to-all-start = ((bf16[8,208,512]{2,1,0:T(8,128)(2,1)}), bf16[8,208,512]{2,1,0:T(8,128)(2,1)S(1)}, u32[]{:S(2)}, u32[]{:S(2)}) async-start(bf16[8,208,512]{2,1,0:T(8,128)(2,1)} %get-tuple-element.119), calls=%async_computation | async-start | bytes 3407872 | tf_op jit(solution)/shard_map/all_to_all | solution.py:1122
  10.1 2.8 collective-permute-start.3
  13.9 1.8 collective-permute-start.4
  15.7 2.9 collective-permute-start
  19.3 3.6 %collective-permute-start.7 = (bf16[208,512]{1,0:T(8,128)(2,1)}, bf16[208,512]{1,0:T(8,128)(2,1)S(1)}, u32[]{:S(2)}, u32[]{:S(2)}) collective-permute-start(bf16[208,512]{1,0:T(8,128)(2,1)} %collective-permute-done.3.refs_3_), channel_id=1, source_target_pairs={{0,2},{2,0},{1,3},{3,1},{4,6},{6,4},{5,7},{7,5},{8,10},{10,8},{9,1... | collective-permute-start | bytes 638984 | tf_op jit(solution)/shard_map/ppermute | solution.py:29
  23.9 2.3 collective-permute-done.1.refs_1_
  26.7 4.2 %prepare.1 = (bf16[512,1536]{1,0:T(8,128)(2,1)}, f32[1,1536]{1,0:T(1,128)}, bf16[2,512,384]{2,1,0:T(8,128)(2,1)}, f32[512,128]{1,0:T(8,128)}, bf16[1040,512]{1,0:T(8,128)(2,1)}) custom-call(s32[1]{0:T(128)} %bitcast.1.place, bf16[3,512,256]{2,1,0:T(8,128)(2,1)} %in_weights.1, f32[2,256]{1,0:T(2,128)} %in_biases.1, f32[2,512]{1,0:T(2,128)} %gains.7, ...), custom_call_target="tpu_custom_call" | custom-call | flops 4000000000 | tf_op jit(solution)/shard_map/prepare/pallas_call | solution.py:78
  30.9 2.7 collective-permute-start.13
  35.0 1.2 copy-done.16
  36.2 19.9 %attend.1 = (bf16[192,384]{1,0:T(8,128)(2,1)}, bf16[192,384]{1,0:T(8,128)(2,1)}, bf16[192,384]{1,0:T(8,128)(2,1)}, bf16[192,384]{1,0:T(8,128)(2,1)}, bf16[4,192,...) custom-call(bf16[208,512]{1,0:T(8,128)(2,1)} %get-tuple-element.118., ...), custom_call_target="tpu_custom_call" | custom-call | flops 15000000512 | tf_op jit(solution)/shard_map/attend/pallas_call | solution.py:78
  56.2 1.3 collective-permute-done.13.far_one
  59.2 3.5 %pair_merge.1 = (bf16[192,384]{1,0:T(8,128)(2,1)}, bf16[192,384]{1,0:T(8,128)(2,1)}, bf16[192,384]{1,0:T(8,128)(2,1)}, bf16[192,384]{1,0:T(8,128)(2,1)}) custom-call(bf16[192,384]{1,0:T(8,128)(2,1)} %get-tuple-element.120.refs_0_, bf16[192,384]{1,0:T(8,128)(2,1)} %get-tuple-element.121.refs_1_, bf16[192,384]{1,0:T(8,128)(2,1)} %get-tuple-element.122.refs_2_, ...), custom_call_target="tpu_custom_call" | custom-call | flops 3000000000 | tf_op jit(solution)/shard_map/pair_merge/pallas_call | solution.py:78
  63.0 1.1 collective-permute-start.10
  65.0 1.5 thumbs.1
  66.4 1.8 collective-permute-done.9.refs_1_
  68.2 1.5 collective-permute-done.10.refs_2_
  69.7 3.9 %collective-permute-done.11.refs_3_ = bf16[192,384]{1,0:T(8,128)(2,1)S(1)} collective-permute-done((bf16[192,384]{1,0:T(8,128)(2,1)}, bf16[192,384]{1,0:T(8,128)(2,1)S(1)}, u32[]{:S(2)}, u32[]{:S(2)}) %collective-permute-start.11) | collective-permute-done | bytes 147488 | tf_op jit(solution)/shard_map/ppermute | solution.py:29
  73.7 1.5 merge.1
  75.2 2.0 collective-permute-start.12
  77.2 4.3 %collective-permute-done.12.low_far = bf16[256,256]{1,0:T(8,128)(2,1)S(1)} collective-permute-done((bf16[256,256]{1,0:T(8,128)(2,1)S(1)}, bf16[256,256]{1,0:T(8,128)(2,1)S(1)}, u32[]{:S(2)}, u32[]{:S(2)}) %collective-permute-start.12) | collective-permute-done | bytes 131104 | tf_op jit(solution)/shard_map/ppermute | solution.py:29
  81.6 7.3 %feed_forward.1 = (bf16[256,512]{1,0:T(8,128)(2,1)}, f32[2,256,512]{2,1,0:T(8,128)S(1)}, bf16[2,256,512]{2,1,0:T(8,128)(2,1)S(1)}, bf16[192,640]{1,0:T(8,128)(2,...) custom-call(bf16[256,512]{1,0:T(8,128)(2,1)S(1)} %copy-done, ...), custom_call_target="tpu_custom_call" | custom-call | flops 12000000000 | tf_op jit(solution)/shard_map/feed_forward/pallas_call | solution.py:78
  88.9 1.4 weight_grads.1
  90.3 1.4 collective-permute-start.22
  93.8 4.6 %thumbs_back.1.refs_14_.refs_8_ = bf16[2,2,256,384]{3,2,1,0:T(8,128)(2,1)S(1)} custom-call(s32[1]{0:T(128)} %get-tuple-element.112.counts, bf16[256,1536]{1,0:T(8,128)(2,1)S(1)} %get-tuple-element.147.x, bf16[2,256,512]{2,1,0:T(8,128)(2,1)S(1)} %get-tuple-element.148.mid_low, bf16[256,512]{1,0:T(8,128)(2,1)S(1)} %copy-done.4), custom_call_target="tpu_custom_call" | custom-call | flops 6000000000 | tf_op jit(solution)/shard_map/thumbs_back/pallas_call | solution.py:78
  99.0 2.1 collective-permute-start.21
  101.1 2.1 collective-permute-start.20
  103.1 3.6 %collective-permute-done.15.refs_1_ = bf16[192,640]{1,0:T(8,128)(2,1)S(1)} collective-permute-done((bf16[192,640]{1,0:T(8,128)(2,1)S(1)}, bf16[192,640]{1,0:T(8,128)(2,1)S(1)}, u32[]{:S(2)}, u32[]{:S(2)}) %collective-permute-start.15) | collective-permute-done | bytes 245792 | tf_op jit(solution)/shard_map/ppermute | solution.py:29
  107.6 2.0 add_convert_fusion
  110.5 7.6 %all-to-all-start.1 = ((bf16[16,32,2304]{2,1,0:T(8,128)(2,1)}), bf16[16,32,2304]{2,1,0:T(8,128)(2,1)S(1)}, u32[]{:S(2)}, u32[]{:S(2)}) async-start(bf16[16,32,2304]{2,1,0:T(8,128)(2,1)} %add_convert_fusion), calls=%async_computation.1 | async-start | bytes 4718592 | tf_op jit(solution)/shard_map/all_to_all | solution.py:1156
  118.1 40.6 %reverse.1 = (bf16[192,512]{1,0:T(8,128)(2,1)}, bf16[192,512]{1,0:T(8,128)(2,1)}, bf16[192,512]{1,0:T(8,128)(2,1)}, bf16[192,512]{1,0:T(8,128)(2,1)}, bf16[4,192...) custom-call(s32[16]{0:T(128)} %get-tuple-element.136.counts, ...), custom_call_target="tpu_custom_call" | custom-call | flops 44999999488 | tf_op jit(solution)/shard_map/reverse/pallas_call | solution.py:78
  158.7 2.8 collective-permute-start.23
  161.5 2.7 collective-permute-start.26
  165.2 11.5 %collective-permute-start.24 = (bf16[32,2304]{1,0:T(8,128)(2,1)S(1)}, bf16[32,2304]{1,0:T(8,128)(2,1)S(1)}, u32[]{:S(2)}, u32[]{:S(2)}) collective-permute-start(bf16[32,2304]{1,0:T(8,128)(2,1)S(1)} %reduce_sum.24), channel_id=1, source_target_pairs={{0,16},{16,0},{1,17},{17,1},{2,18},{18,2},{3,19},{19,3},{4,20},{20... | collective-permute-start | bytes 442376 | tf_op jit(solution)/shard_map/ppermute | solution.py:29
  176.7 2.9 add_convert_fusion.1
  179.6 1.3 collective-permute-done.24
  181.8 3.5 %all-to-all-start.2 = ((bf16[4,32,2304]{2,1,0:T(8,128)(2,1)}), bf16[4,32,2304]{2,1,0:T(8,128)(2,1)S(1)}, u32[]{:S(2)}, u32[]{:S(2)}) async-start(bf16[4,32,2304]{2,1,0:T(8,128)(2,1)} %broadcast_in_dim.28), calls=%async_computation.2 | async-start | bytes 1179648 | tf_op jit(solution)/shard_map/all_to_all | solution.py:1166
  185.3 2.5 fold.1
  187.8 2.4 collective-permute-start.28
  191.1 3.6 %collective-permute-done.28.refs_1_ = bf16[192,512]{1,0:T(8,128)(2,1)S(1)} collective-permute-done((bf16[192,512]{1,0:T(8,128)(2,1)}, bf16[192,512]{1,0:T(8,128)(2,1)S(1)}, u32[]{:S(2)}, u32[]{:S(2)}) %collective-permute-start.28) | collective-permute-done | bytes 196640 | tf_op jit(solution)/shard_map/ppermute | solution.py:29
  194.8 2.6 collective-permute-done.29.refs_2_
  198.1 4.9 %collective-permute-done.30.refs_3_ = bf16[192,512]{1,0:T(8,128)(2,1)} collective-permute-done((bf16[192,512]{1,0:T(8,128)(2,1)}, bf16[192,512]{1,0:T(8,128)(2,1)}, u32[]{:S(2)}, u32[]{:S(2)}) %collective-permute-start.30) | collective-permute-done | bytes 196640 | tf_op jit(solution)/shard_map/ppermute | solution.py:29
  203.0 4.5 %all-to-all-start.3 = ((bf16[16,32,1024]{2,1,0:T(8,128)(2,1)}), bf16[16,32,1024]{2,1,0:T(8,128)(2,1)S(1)}, u32[]{:S(2)}, u32[]{:S(2)}) async-start(bf16[16,32,1024]{2,1,0:T(8,128)(2,1)} %bitcast.13), calls=%async_computation.3 | async-start | bytes 2097152 | tf_op jit(solution)/shard_map/all_to_all | solution.py:1174
  207.5 2.6 collective-permute-start.36
  210.1 2.7 collective-permute-start.31
  212.8 20.3 %collective-permute-done.36.refs_3_ = bf16[4,32,2304]{2,1,0:T(8,128)(2,1)S(1)} collective-permute-done((bf16[4,32,2304]{2,1,0:T(8,128)(2,1)S(1)}, bf16[4,32,2304]{2,1,0:T(8,128)(2,1)S(1)}, u32[]{:S(2)}, u32[]{:S(2)}) %collective-permute-start.36) | collective-permute-done | bytes 589856 | tf_op jit(solution)/shard_map/ppermute | solution.py:29
  233.9 1.2 collective-permute-done.35.refs_1_
  235.3 2.4 collective-permute-start.39
  238.2 1.7 collective-permute-start.43
  240.5 1.3 collective-permute-done.38
  241.8 1.4 collective-permute-done.37
  243.3 1.1 broadcast_in_dim.32
  244.4 5.0 %all-to-all-start.4 = ((bf16[16,32,1024]{2,1,0:T(8,128)(2,1)}), bf16[16,32,1024]{2,1,0:T(8,128)(2,1)S(1)}, u32[]{:S(2)}, u32[]{:S(2)}) async-start(bf16[16,32,1024]{2,1,0:T(8,128)(2,1)} %broadcast_in_dim.32), calls=%async_computation.4 | async-start | bytes 2097152 | tf_op jit(solution)/shard_map/all_to_all | solution.py:1181
  249.4 5.4 %grad_one.1 = (bf16[2,256,512]{2,1,0:T(8,128)(2,1)}, bf16[2,192,512]{2,1,0:T(8,128)(2,1)}) custom-call(s32[1]{0:T(128)} %get-tuple-element.112.counts, bf16[192,512]{1,0:T(8,128)(2,1)} %get-tuple-element.183.refs_0_, bf16[192,512]{1,0:T(8,128)(2,1)} %copy-done.39, bf16[192,512]{1,0:T(8,128)(2,1)} %copy-done.40, ...), custom_call_target="tpu_custom_call" | custom-call | flops 5000000000 | tf_op jit(solution)/shard_map/grad_one/pallas_call | solution.py:78
  254.8 2.5 collective-permute-start.32
  257.9 5.7 %collective-permute-start.41 = (bf16[4,32,2304]{2,1,0:T(8,128)(2,1)S(1)}, bf16[4,32,2304]{2,1,0:T(8,128)(2,1)S(1)}, u32[]{:S(2)}, u32[]{:S(2)}) collective-permute-start(bf16[4,32,2304]{2,1,0:T(8,128)(2,1)S(1)} %all-to-all-done.2.refs_0_), channel_id=1, source_target_pairs={{0,2},{2,0},{1,3},{3,1},{4,6},{6,4},{5,7},{7,5},{8,10},{10,8},{9,1... | collective-permute-start | bytes 1769480 | tf_op jit(solution)/shard_map/ppermute | solution.py:29
  263.7 14.2 %collective-permute-done.34.cross = bf16[2,192,512]{2,1,0:T(8,128)(2,1)S(1)} collective-permute-done((bf16[2,192,512]{2,1,0:T(8,128)(2,1)}, bf16[2,192,512]{2,1,0:T(8,128)(2,1)S(1)}, u32[]{:S(2)}, u32[]{:S(2)}) %collective-permute-start.34) | collective-permute-done | bytes 393248 | tf_op jit(solution)/shard_map/ppermute | solution.py:1083
  277.9 1.6 collective-permute-start.42
  280.5 4.2 %close.1 = f32[2,256,512]{2,1,0:T(8,128)} custom-call(s32[1]{0:T(128)} %get-tuple-element.112.counts, bf16[256,512]{1,0:T(8,128)(2,1)} %tokens.7, f32[2,256,512]{2,1,0:T(8,128)} %copy-done.10, bf16[2,256,512]{2,1,0:T(8,128)(2,1)} %get-tuple-element.191.mine, bf16[2,256,512]{2,1,0:T(8,128)(2,1)} %copy-done.26, bf16[2,192,512]{2,1,0:T(8,128)(2,1)} %copy-done.28, ...), custom_call_target="tpu_custom_call" | custom-call | flops 4000000000 | tf_op jit(solution)/shard_map/close/pallas_call | solution.py:78
  285.1 4.2 %early_own.1 = (f32[2,1024,512]{2,1,0:T(8,128)}, f32[2,512,1024]{2,1,0:T(8,128)}, f32[2,256,512]{2,1,0:T(8,128)}) custom-call(s32[11]{0:T(128)} %stack.44.place, bf16[4,32,2304]{2,1,0:T(8,128)(2,1)} %copy-done.18, bf16[4,32,2304]{2,1,0:T(8,128)(2,1)} %collective-permute-done.35.refs_1_, bf16[4,32,2304]{2,1,0:T(8,128)(2,1)} %collective-permute-done.43.refs_2_, ...), custom_call_target="tpu_custom_call" | custom-call | flops 5000000000 | tf_op jit(solution)/shard_map/early_own/pallas_call | solution.py:989
  290.2 4.2 %early_far.1 = (f32[2,1024,512]{2,1,0:T(8,128)}, f32[2,512,1024]{2,1,0:T(8,128)}, f32[2,256,512]{2,1,0:T(8,128)}) custom-call(s32[11]{0:T(128)} %stack.44.place, bf16[4,32,2304]{2,1,0:T(8,128)(2,1)} %copy-done.24, bf16[4,32,2304]{2,1,0:T(8,128)(2,1)} %collective-permute-done.42.refs_1_, ...), custom_call_target="tpu_custom_call", output_to_operand_aliasing={{0}: (5, {}), {1}: (6, {}), {2}: (7, {})} | custom-call | flops 5000000000 | tf_op jit(solution)/shard_map/early_far/pallas_call | solution.py:989
  294.4 2.6 late_own.1
  298.0 2.6 late_far.1
  300.7 1.3 copy.31
  (153 shorter events, 21.6 us)
Async XLA Ops:
  0.6 15.1 %copy-start.4 = (bf16[256,512]{1,0:T(8,128)(2,1)S(1)}, bf16[256,512]{1,0:T(8,128)(2,1)}, u32[]{:S(2)}) copy-start(bf16[256,512]{1,0:T(8,128)(2,1)} %out_weight.3) | copy-start | bytes 786436
  3.1 31.9 %all-to-all-start = ((bf16[8,208,512]{2,1,0:T(8,128)(2,1)}), bf16[8,208,512]{2,1,0:T(8,128)(2,1)S(1)}, u32[]{:S(2)}, u32[]{:S(2)}) async-start(bf16[8,208,512]{2,1,0:T(8,128)(2,1)} %get-tuple-element.119), calls=%async_computation | async-start | bytes 3407872 | tf_op jit(solution)/shard_map/all_to_all | solution.py:1122
  10.1 9.2 %collective-permute-start.3 = (bf16[208,512]{1,0:T(8,128)(2,1)S(1)}, bf16[208,512]{1,0:T(8,128)(2,1)}, u32[]{:S(2)}, u32[]{:S(2)}) collective-permute-start(bf16[208,512]{1,0:T(8,128)(2,1)S(1)} %copy-done.36), channel_id=1, source_target_pairs={{0,12},{4,0},{8,4},{12,8},{1,13},{5,1},{9,5},{13,9},{2,14},{6,2},{... | collective-permute-start | bytes 638984 | tf_op jit(solution)/shard_map/ppermute | solution.py:29
  12.9 10.0 %collective-permute-start.2 = (bf16[208,512]{1,0:T(8,128)(2,1)S(1)}, bf16[208,512]{1,0:T(8,128)(2,1)}, u32[]{:S(2)}, u32[]{:S(2)}) collective-permute-start(bf16[208,512]{1,0:T(8,128)(2,1)S(1)} %copy-done.36), channel_id=1, source_target_pairs={{0,8},{4,12},{8,0},{12,4},{1,9},{5,13},{9,1},{13,5},{2,10},{6,14},... | collective-permute-start | bytes 638984 | tf_op jit(solution)/shard_map/ppermute | solution.py:29
  13.2 13.0 %collective-permute-start.1 = (bf16[208,512]{1,0:T(8,128)(2,1)S(1)}, bf16[208,512]{1,0:T(8,128)(2,1)}, u32[]{:S(2)}, u32[]{:S(2)}) collective-permute-start(bf16[208,512]{1,0:T(8,128)(2,1)S(1)} %copy-done.36), channel_id=1, source_target_pairs={{0,4},{4,8},{8,12},{12,0},{1,5},{5,9},{9,13},{13,1},{2,6},{6,10},{... | collective-permute-start | bytes 638984 | tf_op jit(solution)/shard_map/ppermute | solution.py:29
  13.9 19.7 %collective-permute-start.4 = (bf16[208,512]{1,0:T(8,128)(2,1)S(1)}, bf16[208,512]{1,0:T(8,128)(2,1)}, u32[]{:S(2)}, u32[]{:S(2)}) collective-permute-start(bf16[208,512]{1,0:T(8,128)(2,1)S(1)} %copy-done.36), channel_id=1, source_target_pairs={{0,2},{2,0},{1,3},{3,1},{4,6},{6,4},{5,7},{7,5},{8,10},{10,8},{9,1... | collective-permute-start | bytes 638984 | tf_op jit(solution)/shard_map/ppermute | solution.py:29
  15.7 15.2 %collective-permute-start = (bf16[256,512]{1,0:T(8,128)(2,1)S(1)}, bf16[256,512]{1,0:T(8,128)(2,1)S(1)}, u32[]{:S(2)}, u32[]{:S(2)}) collective-permute-start(bf16[256,512]{1,0:T(8,128)(2,1)S(1)} %copy-done.4), channel_id=1, source_target_pairs={{0,17},{1,16},{16,1},{17,0},{2,19},{3,18},{18,3},{19,2},{4,21},{5,... | collective-permute-start | bytes 786440 | tf_op jit(solution)/shard_map/ppermute | solution.py:1083
  19.3 14.3 %collective-permute-start.7 = (bf16[208,512]{1,0:T(8,128)(2,1)}, bf16[208,512]{1,0:T(8,128)(2,1)S(1)}, u32[]{:S(2)}, u32[]{:S(2)}) collective-permute-start(bf16[208,512]{1,0:T(8,128)(2,1)} %collective-permute-done.3.refs_3_), channel_id=1, source_target_pairs={{0,2},{2,0},{1,3},{3,1},{4,6},{6,4},{5,7},{7,5},{8,10},{10,8},{9,1... | collective-permute-start | bytes 638984 | tf_op jit(solution)/shard_map/ppermute | solution.py:29
  22.9 10.7 %collective-permute-start.6 = (bf16[208,512]{1,0:T(8,128)(2,1)}, bf16[208,512]{1,0:T(8,128)(2,1)S(1)}, u32[]{:S(2)}, u32[]{:S(2)}) collective-permute-start(bf16[208,512]{1,0:T(8,128)(2,1)} %collective-permute-done.2.refs_2_), channel_id=1, source_target_pairs={{0,2},{2,0},{1,3},{3,1},{4,6},{6,4},{5,7},{7,5},{8,10},{10,8},{9,1... | collective-permute-start | bytes 638984 | tf_op jit(solution)/shard_map/ppermute | solution.py:29
  26.2 8.8 %collective-permute-start.5 = (bf16[208,512]{1,0:T(8,128)(2,1)}, bf16[208,512]{1,0:T(8,128)(2,1)}, u32[]{:S(2)}, u32[]{:S(2)}) collective-permute-start(bf16[208,512]{1,0:T(8,128)(2,1)} %collective-permute-done.1.refs_1_), channel_id=1, source_target_pairs={{0,2},{2,0},{1,3},{3,1},{4,6},{6,4},{5,7},{7,5},{8,10},{10,8},{9,1... | collective-permute-start | bytes 638984 | tf_op jit(solution)/shard_map/ppermute | solution.py:29
  30.9 26.6 %collective-permute-start.13 = (bf16[1040,512]{1,0:T(8,128)(2,1)}, bf16[1040,512]{1,0:T(8,128)(2,1)S(1)}, u32[]{:S(2)}, u32[]{:S(2)}) collective-permute-start(bf16[1040,512]{1,0:T(8,128)(2,1)} %get-tuple-element.133), channel_id=1, source_target_pairs={{0,17},{1,16},{16,1},{17,0},{2,19},{3,18},{18,3},{19,2},{4,21},{5,... | collective-permute-start | bytes 3194888 | tf_op jit(solution)/shard_map/ppermute | solution.py:1083
  56.1 2.3 collective-permute-start.8
  57.5 19.8 %collective-permute-start.14 = (bf16[1040,512]{1,0:T(8,128)(2,1)S(1)}, bf16[1040,512]{1,0:T(8,128)(2,1)S(1)}, u32[]{:S(2)}, u32[]{:S(2)}) collective-permute-start(bf16[1040,512]{1,0:T(8,128)(2,1)S(1)} %collective-permute-done.13.far_one), channel_id=1, source_target_pairs={{0,2},{2,0},{1,3},{3,1},{4,6},{6,4},{5,7},{7,5},{8,10},{10,8},{9,1... | collective-permute-start | bytes 3194888 | tf_op jit(solution)/shard_map/ppermute | solution.py:29
  62.7 5.5 %collective-permute-start.9 = (bf16[192,384]{1,0:T(8,128)(2,1)}, bf16[192,384]{1,0:T(8,128)(2,1)S(1)}, u32[]{:S(2)}, u32[]{:S(2)}) collective-permute-start(bf16[192,384]{1,0:T(8,128)(2,1)} %get-tuple-element.126), channel_id=1, source_target_pairs={{0,12},{4,0},{8,4},{12,8},{1,13},{5,1},{9,5},{13,9},{2,14},{6,2},{... | collective-permute-start | bytes 442376 | tf_op jit(solution)/shard_map/ppermute | solution.py:29
  63.0 6.7 %collective-permute-start.10 = (bf16[192,384]{1,0:T(8,128)(2,1)}, bf16[192,384]{1,0:T(8,128)(2,1)S(1)}, u32[]{:S(2)}, u32[]{:S(2)}) collective-permute-start(bf16[192,384]{1,0:T(8,128)(2,1)} %get-tuple-element.127), channel_id=1, source_target_pairs={{0,8},{4,12},{8,0},{12,4},{1,9},{5,13},{9,1},{13,5},{2,10},{6,14},... | collective-permute-start | bytes 442376 | tf_op jit(solution)/shard_map/ppermute | solution.py:29
  64.1 9.6 %copy-start.12 = (bf16[192,384]{1,0:T(8,128)(2,1)S(1)}, bf16[192,384]{1,0:T(8,128)(2,1)}, u32[]{:S(2)}) copy-start(bf16[192,384]{1,0:T(8,128)(2,1)} %get-tuple-element.125.refs_0_) | copy-start | bytes 442372
  64.1 9.6 %collective-permute-start.11 = (bf16[192,384]{1,0:T(8,128)(2,1)}, bf16[192,384]{1,0:T(8,128)(2,1)S(1)}, u32[]{:S(2)}, u32[]{:S(2)}) collective-permute-start(bf16[192,384]{1,0:T(8,128)(2,1)} %get-tuple-element.128), channel_id=1, source_target_pairs={{0,4},{4,8},{8,12},{12,0},{1,5},{5,9},{9,13},{13,1},{2,6},{6,10},{... | collective-permute-start | bytes 442376 | tf_op jit(solution)/shard_map/ppermute | solution.py:29
  66.4 8.8 %copy-start.13 = (bf16[256,512]{1,0:T(8,128)(2,1)}, bf16[256,512]{1,0:T(8,128)(2,1)S(1)}, u32[]{:S(2)}) copy-start(bf16[256,512]{1,0:T(8,128)(2,1)S(1)} %get-tuple-element.162.refs_13_) | copy-start | bytes 786436
  73.7 7.9 %copy-start.2 = (bf16[1024,512]{1,0:T(8,128)(2,1)S(1)}, bf16[1024,512]{1,0:T(8,128)(2,1)}, u32[]{:S(2)}) copy-start(bf16[1024,512]{1,0:T(8,128)(2,1)} %down.3) | copy-start | bytes 3145732
  73.7 7.9 %copy-start.3 = (bf16[2,256,512]{2,1,0:T(8,128)(2,1)S(1)}, bf16[2,256,512]{2,1,0:T(8,128)(2,1)}, u32[]{:S(2)}) copy-start(bf16[2,256,512]{2,1,0:T(8,128)(2,1)} %outer.3) | copy-start | bytes 1572868
  75.2 6.4 %collective-permute-start.12 = (bf16[256,256]{1,0:T(8,128)(2,1)S(1)}, bf16[256,256]{1,0:T(8,128)(2,1)S(1)}, u32[]{:S(2)}, u32[]{:S(2)}) collective-permute-start(bf16[256,256]{1,0:T(8,128)(2,1)S(1)} %get-tuple-element.129.low), channel_id=1, source_target_pairs={{0,1},{1,0},{2,3},{3,2},{4,5},{5,4},{6,7},{7,6},{8,9},{9,8},{10,11... | collective-permute-start | bytes 393224 | tf_op jit(solution)/shard_map/ppermute | solution.py:29
  90.3 17.2 %collective-permute-start.22 = (bf16[16,32,2304]{2,1,0:T(8,128)(2,1)S(1)}, bf16[16,32,2304]{2,1,0:T(8,128)(2,1)S(1)}, u32[]{:S(2)}, u32[]{:S(2)}) collective-permute-start(bf16[16,32,2304]{2,1,0:T(8,128)(2,1)S(1)} %get-tuple-element.146), channel_id=1, source_target_pairs={{0,2},{2,0},{1,3},{3,1},{4,6},{6,4},{5,7},{7,5},{8,10},{10,8},{9,1... | collective-permute-start | bytes 7077896 | tf_op jit(solution)/shard_map/ppermute | solution.py:29
  91.8 17.8 %collective-permute-start.18 = (bf16[192,640]{1,0:T(8,128)(2,1)S(1)}, bf16[192,640]{1,0:T(8,128)(2,1)S(1)}, u32[]{:S(2)}, u32[]{:S(2)}) collective-permute-start(bf16[192,640]{1,0:T(8,128)(2,1)S(1)} %get-tuple-element.149.refs_0_), channel_id=1, source_target_pairs={{0,2},{2,0},{1,3},{3,1},{4,6},{6,4},{5,7},{7,5},{8,10},{10,8},{9,1... | collective-permute-start | bytes 737288 | tf_op jit(solution)/shard_map/ppermute | solution.py:29
  91.8 7.1 %collective-permute-start.17 = (bf16[192,640]{1,0:T(8,128)(2,1)S(1)}, bf16[192,640]{1,0:T(8,128)(2,1)S(1)}, u32[]{:S(2)}, u32[]{:S(2)}) collective-permute-start(bf16[192,640]{1,0:T(8,128)(2,1)S(1)} %get-tuple-element.149.refs_0_), channel_id=1, source_target_pairs={{0,12},{4,0},{8,4},{12,8},{1,13},{5,1},{9,5},{13,9},{2,14},{6,2},{... | collective-permute-start | bytes 737288 | tf_op jit(solution)/shard_map/ppermute | solution.py:29
  92.0 9.0 %collective-permute-start.16 = (bf16[192,640]{1,0:T(8,128)(2,1)S(1)}, bf16[192,640]{1,0:T(8,128)(2,1)S(1)}, u32[]{:S(2)}, u32[]{:S(2)}) collective-permute-start(bf16[192,640]{1,0:T(8,128)(2,1)S(1)} %get-tuple-element.149.refs_0_), channel_id=1, source_target_pairs={{0,8},{4,12},{8,0},{12,4},{1,9},{5,13},{9,1},{13,5},{2,10},{6,14},... | collective-permute-start | bytes 737288 | tf_op jit(solution)/shard_map/ppermute | solution.py:29
  92.9 13.8 %collective-permute-start.15 = (bf16[192,640]{1,0:T(8,128)(2,1)S(1)}, bf16[192,640]{1,0:T(8,128)(2,1)S(1)}, u32[]{:S(2)}, u32[]{:S(2)}) collective-permute-start(bf16[192,640]{1,0:T(8,128)(2,1)S(1)} %get-tuple-element.149.refs_0_), channel_id=1, source_target_pairs={{0,4},{4,8},{8,12},{12,0},{1,5},{5,9},{9,13},{13,1},{2,6},{6,10},{... | collective-permute-start | bytes 737288 | tf_op jit(solution)/shard_map/ppermute | solution.py:29
  98.4 11.2 %copy-start.11 = (bf16[2,2,256,384]{3,2,1,0:T(8,128)(2,1)}, bf16[2,2,256,384]{3,2,1,0:T(8,128)(2,1)S(1)}, u32[]{:S(2)}) copy-start(bf16[2,2,256,384]{3,2,1,0:T(8,128)(2,1)S(1)} %thumbs_back.1.refs_14_.refs_8_) | copy-start | bytes 2359300
  99.0 10.6 %copy-start.30 = (bf16[192,640]{1,0:T(8,128)(2,1)}, bf16[192,640]{1,0:T(8,128)(2,1)S(1)}, u32[]{:S(2)}) copy-start(bf16[192,640]{1,0:T(8,128)(2,1)S(1)} %collective-permute-done.17.refs_3_) | copy-start | bytes 737284
  99.0 10.6 %collective-permute-start.21 = (bf16[192,640]{1,0:T(8,128)(2,1)S(1)}, bf16[192,640]{1,0:T(8,128)(2,1)S(1)}, u32[]{:S(2)}, u32[]{:S(2)}) collective-permute-start(bf16[192,640]{1,0:T(8,128)(2,1)S(1)} %collective-permute-done.17.refs_3_), channel_id=1, source_target_pairs={{0,2},{2,0},{1,3},{3,1},{4,6},{6,4},{5,7},{7,5},{8,10},{10,8},{9,1... | collective-permute-start | bytes 737288 | tf_op jit(solution)/shard_map/ppermute | solution.py:29
  101.1 8.5 %copy-start.31 = (bf16[192,640]{1,0:T(8,128)(2,1)}, bf16[192,640]{1,0:T(8,128)(2,1)S(1)}, u32[]{:S(2)}) copy-start(bf16[192,640]{1,0:T(8,128)(2,1)S(1)} %collective-permute-done.16.refs_2_) | copy-start | bytes 737284
  101.1 8.6 %collective-permute-start.20 = (bf16[192,640]{1,0:T(8,128)(2,1)S(1)}, bf16[192,640]{1,0:T(8,128)(2,1)S(1)}, u32[]{:S(2)}, u32[]{:S(2)}) collective-permute-start(bf16[192,640]{1,0:T(8,128)(2,1)S(1)} %collective-permute-done.16.refs_2_), channel_id=1, source_target_pairs={{0,2},{2,0},{1,3},{3,1},{4,6},{6,4},{5,7},{7,5},{8,10},{10,8},{9,1... | collective-permute-start | bytes 737288 | tf_op jit(solution)/shard_map/ppermute | solution.py:29
  106.7 3.0 collective-permute-start.19
  110.5 54.3 %all-to-all-start.1 = ((bf16[16,32,2304]{2,1,0:T(8,128)(2,1)}), bf16[16,32,2304]{2,1,0:T(8,128)(2,1)S(1)}, u32[]{:S(2)}, u32[]{:S(2)}) async-start(bf16[16,32,2304]{2,1,0:T(8,128)(2,1)} %add_convert_fusion), calls=%async_computation.1 | async-start | bytes 4718592 | tf_op jit(solution)/shard_map/all_to_all | solution.py:1156
  158.7 18.0 %collective-permute-start.23 = (bf16[512,1024]{1,0:T(8,128)(2,1)}, bf16[512,1024]{1,0:T(8,128)(2,1)}, u32[]{:S(2)}, u32[]{:S(2)}) collective-permute-start(bf16[512,1024]{1,0:T(8,128)(2,1)} %get-tuple-element.168), channel_id=1, source_target_pairs={{0,2},{2,0},{1,3},{3,1},{4,6},{6,4},{5,7},{7,5},{8,10},{10,8},{9,1... | collective-permute-start | bytes 3145736 | tf_op jit(solution)/shard_map/ppermute | solution.py:29
  161.5 29.6 %collective-permute-start.25 = (bf16[2,192,1024]{2,1,0:T(8,128)(2,1)}, bf16[2,192,1024]{2,1,0:T(8,128)(2,1)S(1)}, u32[]{:S(2)}, u32[]{:S(2)}) collective-permute-start(bf16[2,192,1024]{2,1,0:T(8,128)(2,1)} %get-tuple-element.172), channel_id=1, source_target_pairs={{0,32},{32,64},{64,96},{96,0},{1,33},{33,65},{65,97},{97,1},{2,34}... | collective-permute-start | bytes 2359304 | tf_op jit(solution)/shard_map/ppermute | solution.py:29
  161.5 29.6 %collective-permute-start.26 = (bf16[2,192,1024]{2,1,0:T(8,128)(2,1)}, bf16[2,192,1024]{2,1,0:T(8,128)(2,1)}, u32[]{:S(2)}, u32[]{:S(2)}) collective-permute-start(bf16[2,192,1024]{2,1,0:T(8,128)(2,1)} %get-tuple-element.173), channel_id=1, source_target_pairs={{0,96},{32,0},{64,32},{96,64},{1,97},{33,1},{65,33},{97,65},{2,98}... | collective-permute-start | bytes 2359304 | tf_op jit(solution)/shard_map/ppermute | solution.py:29
  164.2 21.0 %collective-permute-start.27 = (bf16[4,192,512]{2,1,0:T(8,128)(2,1)}, bf16[4,192,512]{2,1,0:T(8,128)(2,1)}, u32[]{:S(2)}, u32[]{:S(2)}) collective-permute-start(bf16[4,192,512]{2,1,0:T(8,128)(2,1)} %get-tuple-element.178), channel_id=1, source_target_pairs={{0,2},{2,0},{1,3},{3,1},{4,6},{6,4},{5,7},{7,5},{8,10},{10,8},{9,1... | collective-permute-start | bytes 2359304 | tf_op jit(solution)/shard_map/ppermute | solution.py:29
  165.2 15.7 %collective-permute-start.24 = (bf16[32,2304]{1,0:T(8,128)(2,1)S(1)}, bf16[32,2304]{1,0:T(8,128)(2,1)S(1)}, u32[]{:S(2)}, u32[]{:S(2)}) collective-permute-start(bf16[32,2304]{1,0:T(8,128)(2,1)S(1)} %reduce_sum.24), channel_id=1, source_target_pairs={{0,16},{16,0},{1,17},{17,1},{2,18},{18,2},{3,19},{19,3},{4,20},{20... | collective-permute-start | bytes 442376 | tf_op jit(solution)/shard_map/ppermute | solution.py:29
  181.8 21.2 %all-to-all-start.2 = ((bf16[4,32,2304]{2,1,0:T(8,128)(2,1)}), bf16[4,32,2304]{2,1,0:T(8,128)(2,1)S(1)}, u32[]{:S(2)}, u32[]{:S(2)}) async-start(bf16[4,32,2304]{2,1,0:T(8,128)(2,1)} %broadcast_in_dim.28), calls=%async_computation.2 | async-start | bytes 1179648 | tf_op jit(solution)/shard_map/all_to_all | solution.py:1166
  185.3 24.8 %copy-start.20 = (bf16[2,192,1024]{2,1,0:T(8,128)(2,1)S(1)}, bf16[2,192,1024]{2,1,0:T(8,128)(2,1)}, u32[]{:S(2)}) copy-start(bf16[2,192,1024]{2,1,0:T(8,128)(2,1)} %get-tuple-element.189) | copy-start | bytes 2359300
  187.8 7.0 %collective-permute-start.28 = (bf16[192,512]{1,0:T(8,128)(2,1)}, bf16[192,512]{1,0:T(8,128)(2,1)S(1)}, u32[]{:S(2)}, u32[]{:S(2)}) collective-permute-start(bf16[192,512]{1,0:T(8,128)(2,1)} %get-tuple-element.180), channel_id=1, source_target_pairs={{0,12},{4,0},{8,4},{12,8},{1,13},{5,1},{9,5},{13,9},{2,14},{6,2},{... | collective-permute-start | bytes 589832 | tf_op jit(solution)/shard_map/ppermute | solution.py:29
  190.1 7.3 %collective-permute-start.29 = (bf16[192,512]{1,0:T(8,128)(2,1)}, bf16[192,512]{1,0:T(8,128)(2,1)S(1)}, u32[]{:S(2)}, u32[]{:S(2)}) collective-permute-start(bf16[192,512]{1,0:T(8,128)(2,1)} %get-tuple-element.181), channel_id=1, source_target_pairs={{0,8},{4,12},{8,0},{12,4},{1,9},{5,13},{9,1},{13,5},{2,10},{6,14},... | collective-permute-start | bytes 589832 | tf_op jit(solution)/shard_map/ppermute | solution.py:29
  190.7 12.3 %collective-permute-start.30 = (bf16[192,512]{1,0:T(8,128)(2,1)}, bf16[192,512]{1,0:T(8,128)(2,1)}, u32[]{:S(2)}, u32[]{:S(2)}) collective-permute-start(bf16[192,512]{1,0:T(8,128)(2,1)} %get-tuple-element.182), channel_id=1, source_target_pairs={{0,4},{4,8},{8,12},{12,0},{1,5},{5,9},{9,13},{13,1},{2,6},{6,10},{... | collective-permute-start | bytes 589832 | tf_op jit(solution)/shard_map/ppermute | solution.py:29
  191.1 53.3 %copy-start.21 = (bf16[2,192,1024]{2,1,0:T(8,128)(2,1)}, bf16[2,192,1024]{2,1,0:T(8,128)(2,1)S(1)}, u32[]{:S(2)}) copy-start(bf16[2,192,1024]{2,1,0:T(8,128)(2,1)S(1)} %collective-permute-done.25.refs_5_) | copy-start | bytes 2359300
  194.8 40.3 %copy-start.39 = (bf16[192,512]{1,0:T(8,128)(2,1)}, bf16[192,512]{1,0:T(8,128)(2,1)S(1)}, u32[]{:S(2)}) copy-start(bf16[192,512]{1,0:T(8,128)(2,1)S(1)} %collective-permute-done.28.refs_1_) | copy-start | bytes 589828
  203.0 54.9 %copy-start.18 = (bf16[4,32,2304]{2,1,0:T(8,128)(2,1)}, bf16[4,32,2304]{2,1,0:T(8,128)(2,1)S(1)}, u32[]{:S(2)}) copy-start(bf16[4,32,2304]{2,1,0:T(8,128)(2,1)S(1)} %all-to-all-done.2.refs_0_) | copy-start | bytes 1769476
  203.0 32.1 %all-to-all-start.3 = ((bf16[16,32,1024]{2,1,0:T(8,128)(2,1)}), bf16[16,32,1024]{2,1,0:T(8,128)(2,1)S(1)}, u32[]{:S(2)}, u32[]{:S(2)}) async-start(bf16[16,32,1024]{2,1,0:T(8,128)(2,1)} %bitcast.13), calls=%async_computation.3 | async-start | bytes 2097152 | tf_op jit(solution)/shard_map/all_to_all | solution.py:1174
  207.5 25.5 %collective-permute-start.36 = (bf16[4,32,2304]{2,1,0:T(8,128)(2,1)S(1)}, bf16[4,32,2304]{2,1,0:T(8,128)(2,1)S(1)}, u32[]{:S(2)}, u32[]{:S(2)}) collective-permute-start(bf16[4,32,2304]{2,1,0:T(8,128)(2,1)S(1)} %all-to-all-done.2.refs_0_), channel_id=1, source_target_pairs={{0,12},{4,0},{8,4},{12,8},{1,13},{5,1},{9,5},{13,9},{2,14},{6,2},{... | collective-permute-start | bytes 1769480 | tf_op jit(solution)/shard_map/ppermute | solution.py:29
  210.1 25.0 %collective-permute-start.35 = (bf16[4,32,2304]{2,1,0:T(8,128)(2,1)S(1)}, bf16[4,32,2304]{2,1,0:T(8,128)(2,1)}, u32[]{:S(2)}, u32[]{:S(2)}) collective-permute-start(bf16[4,32,2304]{2,1,0:T(8,128)(2,1)S(1)} %all-to-all-done.2.refs_0_), channel_id=1, source_target_pairs={{0,4},{4,8},{8,12},{12,0},{1,5},{5,9},{9,13},{13,1},{2,6},{6,10},{... | collective-permute-start | bytes 1769480 | tf_op jit(solution)/shard_map/ppermute | solution.py:29
  210.1 39.3 %collective-permute-start.31 = (bf16[2,192,1024]{2,1,0:T(8,128)(2,1)S(1)}, bf16[2,192,1024]{2,1,0:T(8,128)(2,1)}, u32[]{:S(2)}, u32[]{:S(2)}) collective-permute-start(bf16[2,192,1024]{2,1,0:T(8,128)(2,1)S(1)} %copy-done.20), channel_id=1, source_target_pairs={{0,64},{32,96},{64,0},{96,32},{1,65},{33,97},{65,1},{97,33},{2,66}... | collective-permute-start | bytes 2359304 | tf_op jit(solution)/shard_map/ppermute | solution.py:29
  235.3 5.2 %collective-permute-start.39 = (bf16[32,256]{1,0:T(8,128)(2,1)S(1)}, bf16[32,256]{1,0:T(8,128)(2,1)S(1)}, u32[]{:S(2)}, u32[]{:S(2)}) collective-permute-start(bf16[32,256]{1,0:T(8,128)(2,1)S(1)} %pad_maximum_fusion), channel_id=1, source_target_pairs={{0,17},{1,16},{16,1},{17,0},{2,19},{3,18},{18,3},{19,2},{4,21},{5,... | collective-permute-start | bytes 49160 | tf_op jit(solution)/shard_map/ppermute | solution.py:1083
  237.7 4.1 %collective-permute-start.38 = (bf16[32,256]{1,0:T(8,128)(2,1)S(1)}, bf16[32,256]{1,0:T(8,128)(2,1)S(1)}, u32[]{:S(2)}, u32[]{:S(2)}) collective-permute-start(bf16[32,256]{1,0:T(8,128)(2,1)S(1)} %pad_maximum_fusion), channel_id=1, source_target_pairs={{0,1},{1,0},{2,3},{3,2},{4,5},{5,4},{6,7},{7,6},{8,9},{9,8},{10,11... | collective-permute-start | bytes 49160 | tf_op jit(solution)/shard_map/ppermute | solution.py:29
  238.2 25.4 %collective-permute-start.43 = (bf16[4,32,2304]{2,1,0:T(8,128)(2,1)S(1)}, bf16[4,32,2304]{2,1,0:T(8,128)(2,1)}, u32[]{:S(2)}, u32[]{:S(2)}) collective-permute-start(bf16[4,32,2304]{2,1,0:T(8,128)(2,1)S(1)} %all-to-all-done.2.refs_0_), channel_id=1, source_target_pairs={{0,8},{4,12},{8,0},{12,4},{1,9},{5,13},{9,1},{13,5},{2,10},{6,14},... | collective-permute-start | bytes 1769480 | tf_op jit(solution)/shard_map/ppermute | solution.py:29
  239.9 3.4 %collective-permute-start.37 = (bf16[32,1024]{1,0:T(8,128)(2,1)S(1)}, bf16[32,1024]{1,0:T(8,128)(2,1)S(1)}, u32[]{:S(2)}, u32[]{:S(2)}) collective-permute-start(bf16[32,1024]{1,0:T(8,128)(2,1)S(1)} %reduce_sum.25), channel_id=1, source_target_pairs={{0,16},{16,0},{1,17},{17,1},{2,18},{18,2},{3,19},{19,3},{4,20},{20... | collective-permute-start | bytes 196616 | tf_op jit(solution)/shard_map/ppermute | solution.py:29
  244.4 40.3 %all-to-all-start.4 = ((bf16[16,32,1024]{2,1,0:T(8,128)(2,1)}), bf16[16,32,1024]{2,1,0:T(8,128)(2,1)S(1)}, u32[]{:S(2)}, u32[]{:S(2)}) async-start(bf16[16,32,1024]{2,1,0:T(8,128)(2,1)} %broadcast_in_dim.32), calls=%async_computation.4 | async-start | bytes 2097152 | tf_op jit(solution)/shard_map/all_to_all | solution.py:1181
  249.4 30.1 %copy-start.23 = (bf16[4,32,2304]{2,1,0:T(8,128)(2,1)S(1)}, bf16[4,32,2304]{2,1,0:T(8,128)(2,1)}, u32[]{:S(2)}) copy-start(bf16[4,32,2304]{2,1,0:T(8,128)(2,1)} %copy-done.22) | copy-start | bytes 1769476
  254.8 24.8 %collective-permute-start.32 = (bf16[2,256,512]{2,1,0:T(8,128)(2,1)}, bf16[2,256,512]{2,1,0:T(8,128)(2,1)S(1)}, u32[]{:S(2)}, u32[]{:S(2)}) collective-permute-start(bf16[2,256,512]{2,1,0:T(8,128)(2,1)} %get-tuple-element.191.mine), channel_id=1, source_target_pairs={{0,1},{1,0},{2,3},{3,2},{4,5},{5,4},{6,7},{7,6},{8,9},{9,8},{10,11... | collective-permute-start | bytes 1572872 | tf_op jit(solution)/shard_map/ppermute | solution.py:29
  257.4 20.6 %collective-permute-start.34 = (bf16[2,192,512]{2,1,0:T(8,128)(2,1)}, bf16[2,192,512]{2,1,0:T(8,128)(2,1)S(1)}, u32[]{:S(2)}, u32[]{:S(2)}) collective-permute-start(bf16[2,192,512]{2,1,0:T(8,128)(2,1)} %get-tuple-element.192), channel_id=1, source_target_pairs={{0,17},{1,16},{16,1},{17,0},{2,19},{3,18},{18,3},{19,2},{4,21},{5,... | collective-permute-start | bytes 1179656 | tf_op jit(solution)/shard_map/ppermute | solution.py:1083
  257.9 21.6 %collective-permute-start.33 = (bf16[2,192,512]{2,1,0:T(8,128)(2,1)}, bf16[2,192,512]{2,1,0:T(8,128)(2,1)S(1)}, u32[]{:S(2)}, u32[]{:S(2)}) collective-permute-start(bf16[2,192,512]{2,1,0:T(8,128)(2,1)} %get-tuple-element.192), channel_id=1, source_target_pairs={{0,16},{16,0},{1,17},{17,1},{2,18},{18,2},{3,19},{19,3},{4,20},{20... | collective-permute-start | bytes 1179656 | tf_op jit(solution)/shard_map/ppermute | solution.py:29
  257.9 31.4 %collective-permute-start.41 = (bf16[4,32,2304]{2,1,0:T(8,128)(2,1)S(1)}, bf16[4,32,2304]{2,1,0:T(8,128)(2,1)S(1)}, u32[]{:S(2)}, u32[]{:S(2)}) collective-permute-start(bf16[4,32,2304]{2,1,0:T(8,128)(2,1)S(1)} %all-to-all-done.2.refs_0_), channel_id=1, source_target_pairs={{0,2},{2,0},{1,3},{3,1},{4,6},{6,4},{5,7},{7,5},{8,10},{10,8},{9,1... | collective-permute-start | bytes 1769480 | tf_op jit(solution)/shard_map/ppermute | solution.py:29
  263.6 25.8 %collective-permute-start.44 = (bf16[4,32,2304]{2,1,0:T(8,128)(2,1)}, bf16[4,32,2304]{2,1,0:T(8,128)(2,1)}, u32[]{:S(2)}, u32[]{:S(2)}) collective-permute-start(bf16[4,32,2304]{2,1,0:T(8,128)(2,1)} %collective-permute-done.43.refs_2_), channel_id=1, source_target_pairs={{0,2},{2,0},{1,3},{3,1},{4,6},{6,4},{5,7},{7,5},{8,10},{10,8},{9,1... | collective-permute-start | bytes 1769480 | tf_op jit(solution)/shard_map/ppermute | solution.py:29
  277.9 11.5 %collective-permute-start.42 = (bf16[4,32,2304]{2,1,0:T(8,128)(2,1)}, bf16[4,32,2304]{2,1,0:T(8,128)(2,1)}, u32[]{:S(2)}, u32[]{:S(2)}) collective-permute-start(bf16[4,32,2304]{2,1,0:T(8,128)(2,1)} %collective-permute-done.35.refs_1_), channel_id=1, source_target_pairs={{0,2},{2,0},{1,3},{3,1},{4,6},{6,4},{5,7},{7,5},{8,10},{10,8},{9,1... | collective-permute-start | bytes 1769480 | tf_op jit(solution)/shard_map/ppermute | solution.py:29
  279.6 9.9 %collective-permute-start.45 = (bf16[4,32,2304]{2,1,0:T(8,128)(2,1)S(1)}, bf16[4,32,2304]{2,1,0:T(8,128)(2,1)}, u32[]{:S(2)}, u32[]{:S(2)}) collective-permute-start(bf16[4,32,2304]{2,1,0:T(8,128)(2,1)S(1)} %copy-done.23), channel_id=1, source_target_pairs={{0,2},{2,0},{1,3},{3,1},{4,6},{6,4},{5,7},{7,5},{8,10},{10,8},{9,1... | collective-permute-start | bytes 1769480 | tf_op jit(solution)/shard_map/ppermute | solution.py:29
  284.7 12.4 %collective-permute-start.40 = (bf16[512,1024]{1,0:T(8,128)(2,1)S(1)}, bf16[512,1024]{1,0:T(8,128)(2,1)S(1)}, u32[]{:S(2)}, u32[]{:S(2)}) collective-permute-start(bf16[512,1024]{1,0:T(8,128)(2,1)S(1)} %bitcast.20), channel_id=1, source_target_pairs={{0,2},{2,0},{1,3},{3,1},{4,6},{6,4},{5,7},{7,5},{8,10},{10,8},{9,1... | collective-permute-start | bytes 3145736 | tf_op jit(solution)/shard_map/ppermute | solution.py:29
  (28 other events, 79.4 us)
